TPU v7x, 256 devices: a whole 4x4x8 slice. The times are simulated.
256 devices in a mesh: dp: 8 (over y, core), seq: 32 (over z, x).
Axes of the slice: x: 4, y: 4, z: 8, core: 2. Of those that a mesh axis runs over, the one named last changes fastest.
Arguments:
- queries: bfloat16 [8, 4096, 1152], P('dp', 'seq'), may hold values from -12 to 12
- keys: bfloat16 [8, 4096, 1152], P('dp', 'seq'), may hold values from -12 to 12
- values: bfloat16 [8, 4096, 1152], P('dp', 'seq'), may hold values from -6 to 6
- out_weight: bfloat16 [1152, 1152], replicated, may hold values from -0.1875 to 0.1875
- out_grad: bfloat16 [8, 4096, 1152], P('dp', 'seq'), may hold values from -48 to 48
- lengths: int32 [8, 20], P('dp'), may hold values from 128 to 384, as said below
Outputs:
- query_grad: float32 [8, 4096, 1152], P('dp', 'seq')
- key_grad: float32 [8, 4096, 1152], P('dp', 'seq')
- value_grad: float32 [8, 4096, 1152], P('dp', 'seq')
- weight_grad: float32 [1152, 1152], P('seq')
Inputs may be any that keep to these rules, and one draw needn't show every extreme that they name: Each row's 20 lengths sum to 4096; the largest in each row is exactly 384.
All inputs are finite; a program needn't handle non-finite values.
Results may differ from a plain program's by a relative error of at most 0.012.
The roundings to bfloat16 on the way count: a program that leaves them out, or rounds other values in their place, can miss the bound.
Values may be sent and summed in bfloat16 or wider, within the bound.
A program may use at most 128 MiB of HBM per device.

v0:
```python
import math

import jax
import jax.numpy as jnp
from jax import lax
from jax.sharding import PartitionSpec as P

HEADS = 16
HEAD_DIM = 72
MAXLEN = 384


NEG_FILL = -1e30


def shifted(block, axis, distance):
    devices = range(lax.axis_size(axis))
    route = [(i - distance, i) for i in devices if i - distance in devices]
    return lax.ppermute(block, axis, route)


def split_heads(rows_in):
    return rows_in.reshape(rows_in.shape[0], HEADS, HEAD_DIM)


def image_ids(image_ends, shard, tok_rows, shards):
    positions = shard * tok_rows + jnp.arange(tok_rows, dtype=jnp.int32)
    found = jnp.sum((positions[:, None] >= image_ends[None, :]).astype(jnp.int32), axis=1)
    inside = jnp.logical_and(shard >= 0, shard < shards)
    return jnp.where(inside, found, -1)


def masked_scores(q_rows, k_rows, q_ids, k_ids):
    scores = jnp.einsum(
        "qhd,khd->hqk", split_heads(q_rows), split_heads(k_rows), preferred_element_type=jnp.float32
    ) * HEAD_DIM ** (-0.5)
    same_image = q_ids[:, None] == k_ids[None, :]
    return jnp.where(same_image[None, :, :], scores, NEG_FILL)


def touches(q_ids, k_ids):
    return jnp.any(q_ids[:, None] == k_ids[None, :])


def make_probs(q_rows, k_rows, q_ids, k_ids, log_norm):
    return jnp.exp(masked_scores(q_rows, k_rows, q_ids, k_ids) - log_norm[:, :, None]).astype(
        jnp.bfloat16
    )


def score_grads(q_rows, k_rows, v_rows, d_rows, q_ids, k_ids, log_norm, row_delta):
    weights = make_probs(q_rows, k_rows, q_ids, k_ids, log_norm)
    d_probs = jnp.einsum(
        "qhd,khd->hqk", split_heads(d_rows), split_heads(v_rows), preferred_element_type=jnp.float32
    )
    d_scores = (
        HEAD_DIM ** (-0.5) * weights.astype(jnp.float32) * (d_probs - row_delta[:, :, None])
    ).astype(jnp.bfloat16)
    return (weights, d_scores)


def query_part(d_scores, k_rows):
    return jnp.einsum(
        "hqk,khd->qhd", d_scores, split_heads(k_rows), preferred_element_type=jnp.float32
    )


def key_part(weights, d_scores, q_rows, d_rows):
    k_part = jnp.einsum(
        "hqk,qhd->khd", d_scores, split_heads(q_rows), preferred_element_type=jnp.float32
    )
    v_part = jnp.einsum(
        "hqk,qhd->khd", weights, split_heads(d_rows), preferred_element_type=jnp.float32
    )
    return (k_part, v_part)


def body(queries, keys, values, out_weight, out_grad, lengths):
    q_rows = queries[0]
    k_rows = keys[0]
    v_rows = values[0]
    dy_rows = out_grad[0]
    tok_rows = q_rows.shape[0]
    feature_width = q_rows.shape[1]
    shards = lax.axis_size("seq")
    seq_index = lax.axis_index("seq")
    key_reach = (MAXLEN + tok_rows - 2) // tok_rows
    image_ends = jnp.cumsum(lengths[0])
    own_ids = image_ids(image_ends, seq_index, tok_rows, shards)
    d_out = jnp.einsum("td,ed->te", dy_rows, out_weight, preferred_element_type=jnp.float32).astype(
        jnp.bfloat16
    )
    remote = []
    for distance in range(1, key_reach + 1):
        for offset in (distance, -distance):
            arrived = shifted((k_rows, v_rows), "seq", offset)
            remote.append((offset, arrived[0], arrived[1]))
    remote_ids = [image_ids(image_ends, seq_index - entry[0], tok_rows, shards) for entry in remote]
    own_scores = masked_scores(q_rows, k_rows, own_ids, own_ids)
    row_max = jnp.max(own_scores, axis=2)
    row_sum = jnp.sum(jnp.exp(own_scores - row_max[:, :, None]), axis=2)
    for entry, tile_ids in zip(remote, remote_ids):
        k_tile = entry[1]

        def widen(carried):
            old_max, old_sum = carried
            scores = masked_scores(q_rows, k_tile, own_ids, tile_ids)
            new_max = jnp.maximum(old_max, jnp.max(scores, axis=2))
            new_sum = old_sum * jnp.exp(old_max - new_max) + jnp.sum(
                jnp.exp(scores - new_max[:, :, None]), axis=2
            )
            return (new_max, new_sum)

        row_max, row_sum = lax.cond(
            touches(own_ids, tile_ids), widen, lambda carried: carried, (row_max, row_sum)
        )
    log_norm = row_max + jnp.log(row_sum)
    head_zeros = jnp.zeros((tok_rows, HEADS, HEAD_DIM), jnp.float32)
    mixed_sum = jnp.einsum(
        "hqk,khd->qhd",
        make_probs(q_rows, k_rows, own_ids, own_ids, log_norm),
        split_heads(v_rows),
        preferred_element_type=jnp.float32,
    )
    for entry, tile_ids in zip(remote, remote_ids):
        k_tile = entry[1]
        v_tile = entry[2]

        def mix_tile():
            weights = make_probs(q_rows, k_tile, own_ids, tile_ids, log_norm)
            return jnp.einsum(
                "hqk,khd->qhd", weights, split_heads(v_tile), preferred_element_type=jnp.float32
            )

        mixed_sum = mixed_sum + lax.cond(touches(own_ids, tile_ids), mix_tile, lambda: head_zeros)
    attended = mixed_sum.reshape(tok_rows, feature_width).astype(jnp.bfloat16)
    row_delta = jnp.sum(
        (d_out.astype(jnp.float32) * attended.astype(jnp.float32)).reshape(
            tok_rows, HEADS, HEAD_DIM
        ),
        axis=2,
    ).T
    weights, d_scores = score_grads(
        q_rows, k_rows, v_rows, d_out, own_ids, own_ids, log_norm, row_delta
    )
    q_grad = query_part(d_scores, k_rows)
    k_grad, v_grad = key_part(weights, d_scores, q_rows, d_out)
    for entry, tile_ids in zip(remote, remote_ids):
        offset = entry[0]
        k_tile = entry[1]
        v_tile = entry[2]

        def all_parts():
            tile_weights, tile_scores = score_grads(
                q_rows, k_tile, v_tile, d_out, own_ids, tile_ids, log_norm, row_delta
            )
            k_part, v_part = key_part(tile_weights, tile_scores, q_rows, d_out)
            return (query_part(tile_scores, k_tile), k_part, v_part)

        parts = lax.cond(
            touches(own_ids, tile_ids), all_parts, lambda: (head_zeros, head_zeros, head_zeros)
        )
        q_grad = q_grad + parts[0]
        returned = shifted(
            (parts[1].reshape(tok_rows, feature_width), parts[2].reshape(tok_rows, feature_width)),
            "seq",
            -offset,
        )
        k_grad = k_grad + returned[0].reshape(tok_rows, HEADS, HEAD_DIM)
        v_grad = v_grad + returned[1].reshape(tok_rows, HEADS, HEAD_DIM)
    weight_share = lax.psum_scatter(
        jnp.einsum("tr,tc->rc", attended, dy_rows, preferred_element_type=jnp.float32),
        "seq",
        scatter_dimension=0,
        tiled=True,
    )
    weight_sum = lax.psum(weight_share, "dp")
    all_tokens = tok_rows * shards * lax.axis_size("dp")
    weight_grad = weight_sum * (1.0 / math.sqrt(all_tokens))
    return (
        q_grad.reshape(1, tok_rows, feature_width),
        k_grad.reshape(1, tok_rows, feature_width),
        v_grad.reshape(1, tok_rows, feature_width),
        weight_grad,
    )


def solution(mesh):
    in_specs = (
        P("dp", "seq", None),
        P("dp", "seq", None),
        P("dp", "seq", None),
        P(),
        P("dp", "seq", None),
        P("dp", None),
    )
    out_specs = (P("dp", "seq", None), P("dp", "seq", None), P("dp", "seq", None), P("seq", None))
    return jax.shard_map(body, mesh=mesh, in_specs=in_specs, out_specs=out_specs, check_vma=False)
```

profile of v0, /device:TPU:8, one launch (start us, length us, event | category | flops | bytes accessed | tf_op | source)
XLA Modules:
  0.0 408.8 jit_solution(21124440691975372)
XLA Ops:
  8.6 4.1 %collective-permute-start = (bf16[128,1152]{0,1:T(8,128)(2,1)S(1)}, bf16[128,1152]{0,1:T(8,128)(2,1)}, u32[]{:S(2)}, u32[]{:S(2)}) collective-permute-start(bf16[128,1152]{0,1:T(8,128)(2,1)S(1)} %bitcast.261), channel_id=1, source_target_pairs={{0,1},{1,2},{2,3},{3,4},{4,5},{5,6},{6,7},{7,8},{8,9},{9,10},{10,1... | collective-permute-start | bytes 884744 | tf_op jit(solution)/shard_map/ppermute | solution.py:19
  14.0 6.1 %collective-permute-start.2 = (bf16[128,1152]{0,1:T(8,128)(2,1)S(1)}, bf16[128,1152]{0,1:T(8,128)(2,1)}, u32[]{:S(2)}, u32[]{:S(2)}) collective-permute-start(bf16[128,1152]{0,1:T(8,128)(2,1)S(1)} %bitcast.263), channel_id=1, source_target_pairs={{0,2},{1,3},{2,4},{3,5},{4,6},{5,7},{6,8},{7,9},{8,10},{9,11},{10,... | collective-permute-start | bytes 884744 | tf_op jit(solution)/shard_map/ppermute | solution.py:19
  21.4 6.5 %collective-permute-start.4 = (bf16[128,1152]{0,1:T(8,128)(2,1)S(1)}, bf16[128,1152]{0,1:T(8,128)(2,1)}, u32[]{:S(2)}, u32[]{:S(2)}) collective-permute-start(bf16[128,1152]{0,1:T(8,128)(2,1)S(1)} %bitcast.265), channel_id=1, source_target_pairs={{0,3},{1,4},{2,5},{3,6},{4,7},{5,8},{6,9},{7,10},{8,11},{9,12},{10... | collective-permute-start | bytes 884744 | tf_op jit(solution)/shard_map/ppermute | solution.py:19
  46.5 10.1 %collective-permute-start.8 = (bf16[128,1152]{0,1:T(8,128)(2,1)}, bf16[128,1152]{0,1:T(8,128)(2,1)}, u32[]{:S(2)}, u32[]{:S(2)}) collective-permute-start(bf16[128,1152]{0,1:T(8,128)(2,1)} %bitcast.86), channel_id=1, source_target_pairs={{0,2},{1,3},{2,4},{3,5},{4,6},{5,7},{6,8},{7,9},{8,10},{9,11},{10,... | collective-permute-start | bytes 884744 | tf_op jit(solution)/shard_map/ppermute | solution.py:19
  59.7 6.8 %collective-permute-start.10 = (bf16[128,1152]{0,1:T(8,128)(2,1)}, bf16[128,1152]{0,1:T(8,128)(2,1)}, u32[]{:S(2)}, u32[]{:S(2)}) collective-permute-start(bf16[128,1152]{0,1:T(8,128)(2,1)} %bitcast.86), channel_id=1, source_target_pairs={{0,3},{1,4},{2,5},{3,6},{4,7},{5,8},{6,9},{7,10},{8,11},{9,12},{10... | collective-permute-start | bytes 884744 | tf_op jit(solution)/shard_map/ppermute | solution.py:19
  66.5 4.7 %collective-permute-start.6 = (bf16[128,1152]{0,1:T(8,128)(2,1)}, bf16[128,1152]{0,1:T(8,128)(2,1)}, u32[]{:S(2)}, u32[]{:S(2)}) collective-permute-start(bf16[128,1152]{0,1:T(8,128)(2,1)} %bitcast.86), channel_id=1, source_target_pairs={{0,1},{1,2},{2,3},{3,4},{4,5},{5,6},{6,7},{7,8},{8,9},{9,10},{10,1... | collective-permute-start | bytes 884744 | tf_op jit(solution)/shard_map/ppermute | solution.py:19
  75.7 3.0 conditional.27
  87.1 3.2 fusion.106
  90.4 99.9 %fusion = f32[48,1152]{1,0:T(8,128)S(1)} fusion(f32[1152,1152]{1,0:T(8,128)} %fusion.106), kind=kCustom, calls=%all-reduce-scatter | all-reduce-scatter fusion | flops 1769473 | bytes 5530624
  191.1 3.1 collective-permute-start.24
  198.6 7.2 %collective-permute-start.27 = (f32[48,1152]{1,0:T(8,128)S(1)}, f32[48,1152]{1,0:T(8,128)}, u32[]{:S(2)}, u32[]{:S(2)}) collective-permute-start(f32[48,1152]{1,0:T(8,128)S(1)} %fusion), channel_id=1, source_target_pairs={{0,4},{1,5},{2,6},{3,7},{4,8},{5,9},{6,10},{7,11},{8,12},{9,13},{1... | collective-permute-start | bytes 663560
  206.0 14.6 %collective-permute-start.31 = (f32[36,1152]{1,0:T(8,128)}, f32[36,1152]{1,0:T(8,128)}, u32[]{:S(2)}, u32[]{:S(2)}) collective-permute-start(f32[36,1152]{1,0:T(8,128)} %slice), channel_id=1, source_target_pairs={{0,8},{1,9},{2,10},{3,11},{4,12},{5,13},{6,14},{7,15},{8,16},{9,17... | collective-permute-start | bytes 497672
  221.0 9.1 %conditional.31 = (f32[128,16,72]{0,2,1:T(8,128)}, f32[128,16,72]{0,2,1:T(8,128)}, f32[128,16,72]{0,2,1:T(8,128)}) conditional(s32[]{:T(128)} %convert_element_type.160, () %tuple.160, (s32[128]{0:T(128)S(1)}, s32[128]{0:T(128)S(1)}, bf16[1,128,1152]{2,1,0:T(8,128)(2,1)S(1)}, bf16[128,1152]{0,1:T(8,128)(2,1)}, f32[16,128]{1,0:T(8,128)S(1)}, ...), branch_computations={%region_55.56_spmd, %region_56.57_spmd} | conditional | flops 191119360 | bytes 9389108 | solution.py:160
  235.4 9.1 %conditional.33 = (f32[128,16,72]{0,2,1:T(8,128)}, f32[128,16,72]{0,2,1:T(8,128)}, f32[128,16,72]{0,2,1:T(8,128)}) conditional(s32[]{:T(128)} %convert_element_type.156, () %tuple.164, (s32[128]{0:T(128)S(1)}, s32[128]{0:T(128)S(1)}, bf16[1,128,1152]{2,1,0:T(8,128)(2,1)S(1)}, bf16[128,1152]{0,1:T(8,128)(2,1)}, f32[16,128]{1,0:T(8,128)S(1)}, ...), branch_computations={%region_59.60_spmd, %region_60.61_spmd} | conditional | flops 191119360 | bytes 9389108 | solution.py:160
  251.0 2.8 collective-permute-start.19
  255.4 16.9 %collective-permute-start.28 = (f32[48,1152]{1,0:T(8,128)S(1)}, f32[48,1152]{1,0:T(8,128)S(1)}, u32[]{:S(2)}, u32[]{:S(2)}) collective-permute-start(f32[48,1152]{1,0:T(8,128)S(1)} %fusion), channel_id=1, source_target_pairs={{0,5},{1,6},{2,7},{3,8},{4,9},{5,10},{6,11},{7,12},{8,13},{9,14},{... | collective-permute-start | bytes 663560
  274.4 3.3 collective-permute-start.30
  283.1 5.1 %collective-permute-start.21 = (f32[128,1152]{0,1:T(8,128)}, f32[128,1152]{0,1:T(8,128)}, u32[]{:S(2)}, u32[]{:S(2)}) collective-permute-start(f32[128,1152]{0,1:T(8,128)} %bitcast.113), channel_id=1, source_target_pairs={{0,2},{1,3},{2,4},{3,5},{4,6},{5,7},{6,8},{7,9},{8,10},{9,11},{10,... | collective-permute-start | bytes 1769480 | tf_op jit(solution)/shard_map/ppermute | solution.py:19
  289.5 6.6 %collective-permute-start.23 = (f32[128,1152]{0,1:T(8,128)}, f32[128,1152]{0,1:T(8,128)}, u32[]{:S(2)}, u32[]{:S(2)}) collective-permute-start(f32[128,1152]{0,1:T(8,128)} %bitcast.117), channel_id=1, source_target_pairs={{0,3},{1,4},{2,5},{3,6},{4,7},{5,8},{6,9},{7,10},{8,11},{9,12},{10... | collective-permute-start | bytes 1769480 | tf_op jit(solution)/shard_map/ppermute | solution.py:19
  296.1 22.5 %collective-permute-start.13 = (f32[128,1152]{0,1:T(8,128)}, f32[128,1152]{0,1:T(8,128)}, u32[]{:S(2)}, u32[]{:S(2)}) collective-permute-start(f32[128,1152]{0,1:T(8,128)} %bitcast.95), channel_id=1, source_target_pairs={{0,1},{1,2},{2,3},{3,4},{4,5},{5,6},{6,7},{7,8},{8,9},{9,10},{10,1... | collective-permute-start | bytes 1769480 | tf_op jit(solution)/shard_map/ppermute | solution.py:19
  319.1 14.8 %concatenate = f32[420,1152]{1,0:T(8,128)} concatenate(f32[36,1152]{1,0:T(8,128)} %collective-permute-done.31, f32[48,1152]{1,0:T(8,128)} %copy-done.20, f32[48,1152]{1,0:T(8,128)} %copy-done.19, f32[48,1152]{1,0:T(8,128)S(1)} %collective-permute-done.28, f32[48,1152]{1,0:T(8,128)} %collective-permute-done.27, f32[48,1152]{1,0:T(8,128)} %collective-permute-done.26, ...), dimensions={0} | concatenate | bytes 3870720
  340.5 7.6 %collective-permute-start.15 = (f32[128,1152]{0,1:T(8,128)}, f32[128,1152]{0,1:T(8,128)}, u32[]{:S(2)}, u32[]{:S(2)}) collective-permute-start(f32[128,1152]{0,1:T(8,128)} %bitcast.99), channel_id=1, source_target_pairs={{0,2},{1,3},{2,4},{3,5},{4,6},{5,7},{6,8},{7,9},{8,10},{9,11},{10,... | collective-permute-start | bytes 1769480 | tf_op jit(solution)/shard_map/ppermute | solution.py:19
  349.5 6.6 %collective-permute-start.17 = (f32[128,1152]{0,1:T(8,128)}, f32[128,1152]{0,1:T(8,128)}, u32[]{:S(2)}, u32[]{:S(2)}) collective-permute-start(f32[128,1152]{0,1:T(8,128)} %bitcast.103), channel_id=1, source_target_pairs={{0,3},{1,4},{2,5},{3,6},{4,7},{5,8},{6,9},{7,10},{8,11},{9,12},{10... | collective-permute-start | bytes 1769480 | tf_op jit(solution)/shard_map/ppermute | solution.py:19
  356.0 37.5 %all-reduce.4.cloned.1.call-done = f32[36,1152]{1,0:T(8,128)} async-done(((f32[36,1152]{1,0:T(8,128)}), f32[36,1152]{1,0:T(8,128)}) %all-reduce.4.cloned.1.call-update) | async-done | bytes 165904 | tf_op jit(solution)/shard_map/psum | solution.py:177
  (207 shorter events, 117.5 us)
Async XLA Ops:
  7.2 386.4 %all-reduce.4.cloned.1.call-start = ((), (), s32[]{:S(2)}) async-start(), calls=%async_computation | async-start | bytes 368640 | tf_op jit(solution)/shard_map/psum | solution.py:177
  14.0 32.5 %collective-permute-start.2 = (bf16[128,1152]{0,1:T(8,128)(2,1)S(1)}, bf16[128,1152]{0,1:T(8,128)(2,1)}, u32[]{:S(2)}, u32[]{:S(2)}) collective-permute-start(bf16[128,1152]{0,1:T(8,128)(2,1)S(1)} %bitcast.263), channel_id=1, source_target_pairs={{0,2},{1,3},{2,4},{3,5},{4,6},{5,7},{6,8},{7,9},{8,10},{9,11},{10,... | collective-permute-start | bytes 884744 | tf_op jit(solution)/shard_map/ppermute | solution.py:19
  20.1 36.5 %collective-permute-start.3 = (bf16[128,1152]{0,1:T(8,128)(2,1)S(1)}, bf16[128,1152]{0,1:T(8,128)(2,1)}, u32[]{:S(2)}, u32[]{:S(2)}) collective-permute-start(bf16[128,1152]{0,1:T(8,128)(2,1)S(1)} %bitcast.264), channel_id=1, source_target_pairs={{2,0},{3,1},{4,2},{5,3},{6,4},{7,5},{8,6},{9,7},{10,8},{11,9},{12,... | collective-permute-start | bytes 884744 | tf_op jit(solution)/shard_map/ppermute | solution.py:19
  21.4 38.4 %collective-permute-start.4 = (bf16[128,1152]{0,1:T(8,128)(2,1)S(1)}, bf16[128,1152]{0,1:T(8,128)(2,1)}, u32[]{:S(2)}, u32[]{:S(2)}) collective-permute-start(bf16[128,1152]{0,1:T(8,128)(2,1)S(1)} %bitcast.265), channel_id=1, source_target_pairs={{0,3},{1,4},{2,5},{3,6},{4,7},{5,8},{6,9},{7,10},{8,11},{9,12},{10... | collective-permute-start | bytes 884744 | tf_op jit(solution)/shard_map/ppermute | solution.py:19
  35.5 31.0 %collective-permute-start.5 = (bf16[128,1152]{0,1:T(8,128)(2,1)S(1)}, bf16[128,1152]{0,1:T(8,128)(2,1)}, u32[]{:S(2)}, u32[]{:S(2)}) collective-permute-start(bf16[128,1152]{0,1:T(8,128)(2,1)S(1)} %bitcast.266), channel_id=1, source_target_pairs={{3,0},{4,1},{5,2},{6,3},{7,4},{8,5},{9,6},{10,7},{11,8},{12,9},{13... | collective-permute-start | bytes 884744 | tf_op jit(solution)/shard_map/ppermute | solution.py:19
  37.2 34.1 %collective-permute-start.7 = (bf16[128,1152]{0,1:T(8,128)(2,1)}, bf16[128,1152]{0,1:T(8,128)(2,1)}, u32[]{:S(2)}, u32[]{:S(2)}) collective-permute-start(bf16[128,1152]{0,1:T(8,128)(2,1)} %bitcast.86), channel_id=1, source_target_pairs={{1,0},{2,1},{3,2},{4,3},{5,4},{6,5},{7,6},{8,7},{9,8},{10,9},{11,1... | collective-permute-start | bytes 884744 | tf_op jit(solution)/shard_map/ppermute | solution.py:19
  46.5 28.5 %collective-permute-start.8 = (bf16[128,1152]{0,1:T(8,128)(2,1)}, bf16[128,1152]{0,1:T(8,128)(2,1)}, u32[]{:S(2)}, u32[]{:S(2)}) collective-permute-start(bf16[128,1152]{0,1:T(8,128)(2,1)} %bitcast.86), channel_id=1, source_target_pairs={{0,2},{1,3},{2,4},{3,5},{4,6},{5,7},{6,8},{7,9},{8,10},{9,11},{10,... | collective-permute-start | bytes 884744 | tf_op jit(solution)/shard_map/ppermute | solution.py:19
  191.1 62.7 %collective-permute-start.24 = (f32[48,1152]{1,0:T(8,128)S(1)}, f32[48,1152]{1,0:T(8,128)}, u32[]{:S(2)}, u32[]{:S(2)}) collective-permute-start(f32[48,1152]{1,0:T(8,128)S(1)} %fusion), channel_id=1, source_target_pairs={{0,1},{1,2},{2,3},{3,4},{4,5},{5,6},{6,7},{7,8},{8,9},{9,10},{10,1... | collective-permute-start | bytes 663560
  194.2 61.2 %collective-permute-start.25 = (f32[48,1152]{1,0:T(8,128)S(1)}, f32[48,1152]{1,0:T(8,128)}, u32[]{:S(2)}, u32[]{:S(2)}) collective-permute-start(f32[48,1152]{1,0:T(8,128)S(1)} %fusion), channel_id=1, source_target_pairs={{0,2},{1,3},{2,4},{3,5},{4,6},{5,7},{6,8},{7,9},{8,10},{9,11},{10,... | collective-permute-start | bytes 663560
  196.2 76.2 %collective-permute-start.26 = (f32[48,1152]{1,0:T(8,128)S(1)}, f32[48,1152]{1,0:T(8,128)}, u32[]{:S(2)}, u32[]{:S(2)}) collective-permute-start(f32[48,1152]{1,0:T(8,128)S(1)} %fusion), channel_id=1, source_target_pairs={{0,3},{1,4},{2,5},{3,6},{4,7},{5,8},{6,9},{7,10},{8,11},{9,12},{10... | collective-permute-start | bytes 663560
  198.6 75.7 %collective-permute-start.27 = (f32[48,1152]{1,0:T(8,128)S(1)}, f32[48,1152]{1,0:T(8,128)}, u32[]{:S(2)}, u32[]{:S(2)}) collective-permute-start(f32[48,1152]{1,0:T(8,128)S(1)} %fusion), channel_id=1, source_target_pairs={{0,4},{1,5},{2,6},{3,7},{4,8},{5,9},{6,10},{7,11},{8,12},{9,13},{1... | collective-permute-start | bytes 663560
  206.0 44.9 %collective-permute-start.31 = (f32[36,1152]{1,0:T(8,128)}, f32[36,1152]{1,0:T(8,128)}, u32[]{:S(2)}, u32[]{:S(2)}) collective-permute-start(f32[36,1152]{1,0:T(8,128)} %slice), channel_id=1, source_target_pairs={{0,8},{1,9},{2,10},{3,11},{4,12},{5,13},{6,14},{7,15},{8,16},{9,17... | collective-permute-start | bytes 497672
  251.0 38.5 %collective-permute-start.19 = (f32[128,1152]{0,1:T(8,128)}, f32[128,1152]{0,1:T(8,128)S(1)}, u32[]{:S(2)}, u32[]{:S(2)}) collective-permute-start(f32[128,1152]{0,1:T(8,128)} %bitcast.109), channel_id=1, source_target_pairs={{0,1},{1,2},{2,3},{3,4},{4,5},{5,6},{6,7},{7,8},{8,9},{9,10},{10,1... | collective-permute-start | bytes 1769480 | tf_op jit(solution)/shard_map/ppermute | solution.py:19
  253.8 42.3 %collective-permute-start.18 = (f32[128,1152]{0,1:T(8,128)}, f32[128,1152]{0,1:T(8,128)S(1)}, u32[]{:S(2)}, u32[]{:S(2)}) collective-permute-start(f32[128,1152]{0,1:T(8,128)} %bitcast.107), channel_id=1, source_target_pairs={{1,0},{2,1},{3,2},{4,3},{5,4},{6,5},{7,6},{8,7},{9,8},{10,9},{11,1... | collective-permute-start | bytes 1769480 | tf_op jit(solution)/shard_map/ppermute | solution.py:19
  280.0 57.9 %collective-permute-start.20 = (f32[128,1152]{0,1:T(8,128)}, f32[128,1152]{0,1:T(8,128)}, u32[]{:S(2)}, u32[]{:S(2)}) collective-permute-start(f32[128,1152]{0,1:T(8,128)} %bitcast.111), channel_id=1, source_target_pairs={{2,0},{3,1},{4,2},{5,3},{6,4},{7,5},{8,6},{9,7},{10,8},{11,9},{12,... | collective-permute-start | bytes 1769480 | tf_op jit(solution)/shard_map/ppermute | solution.py:19
  283.1 56.2 %collective-permute-start.21 = (f32[128,1152]{0,1:T(8,128)}, f32[128,1152]{0,1:T(8,128)}, u32[]{:S(2)}, u32[]{:S(2)}) collective-permute-start(f32[128,1152]{0,1:T(8,128)} %bitcast.113), channel_id=1, source_target_pairs={{0,2},{1,3},{2,4},{3,5},{4,6},{5,7},{6,8},{7,9},{8,10},{9,11},{10,... | collective-permute-start | bytes 1769480 | tf_op jit(solution)/shard_map/ppermute | solution.py:19
  288.2 52.3 %collective-permute-start.22 = (f32[128,1152]{0,1:T(8,128)}, f32[128,1152]{0,1:T(8,128)}, u32[]{:S(2)}, u32[]{:S(2)}) collective-permute-start(f32[128,1152]{0,1:T(8,128)} %bitcast.115), channel_id=1, source_target_pairs={{3,0},{4,1},{5,2},{6,3},{7,4},{8,5},{9,6},{10,7},{11,8},{12,9},{13... | collective-permute-start | bytes 1769480 | tf_op jit(solution)/shard_map/ppermute | solution.py:19
  289.5 58.6 %collective-permute-start.23 = (f32[128,1152]{0,1:T(8,128)}, f32[128,1152]{0,1:T(8,128)}, u32[]{:S(2)}, u32[]{:S(2)}) collective-permute-start(f32[128,1152]{0,1:T(8,128)} %bitcast.117), channel_id=1, source_target_pairs={{0,3},{1,4},{2,5},{3,6},{4,7},{5,8},{6,9},{7,10},{8,11},{9,12},{10... | collective-permute-start | bytes 1769480 | tf_op jit(solution)/shard_map/ppermute | solution.py:19
  296.1 53.3 %collective-permute-start.13 = (f32[128,1152]{0,1:T(8,128)}, f32[128,1152]{0,1:T(8,128)}, u32[]{:S(2)}, u32[]{:S(2)}) collective-permute-start(f32[128,1152]{0,1:T(8,128)} %bitcast.95), channel_id=1, source_target_pairs={{0,1},{1,2},{2,3},{3,4},{4,5},{5,6},{6,7},{7,8},{8,9},{9,10},{10,1... | collective-permute-start | bytes 1769480 | tf_op jit(solution)/shard_map/ppermute | solution.py:19
  337.9 60.4 %collective-permute-start.12 = (f32[128,1152]{0,1:T(8,128)}, f32[128,1152]{0,1:T(8,128)}, u32[]{:S(2)}, u32[]{:S(2)}) collective-permute-start(f32[128,1152]{0,1:T(8,128)} %bitcast.93), channel_id=1, source_target_pairs={{1,0},{2,1},{3,2},{4,3},{5,4},{6,5},{7,6},{8,7},{9,8},{10,9},{11,1... | collective-permute-start | bytes 1769480 | tf_op jit(solution)/shard_map/ppermute | solution.py:19
  339.2 59.1 %collective-permute-start.14 = (f32[128,1152]{0,1:T(8,128)}, f32[128,1152]{0,1:T(8,128)}, u32[]{:S(2)}, u32[]{:S(2)}) collective-permute-start(f32[128,1152]{0,1:T(8,128)} %bitcast.97), channel_id=1, source_target_pairs={{2,0},{3,1},{4,2},{5,3},{6,4},{7,5},{8,6},{9,7},{10,8},{11,9},{12,... | collective-permute-start | bytes 1769480 | tf_op jit(solution)/shard_map/ppermute | solution.py:19
  340.5 57.8 %collective-permute-start.15 = (f32[128,1152]{0,1:T(8,128)}, f32[128,1152]{0,1:T(8,128)}, u32[]{:S(2)}, u32[]{:S(2)}) collective-permute-start(f32[128,1152]{0,1:T(8,128)} %bitcast.99), channel_id=1, source_target_pairs={{0,2},{1,3},{2,4},{3,5},{4,6},{5,7},{6,8},{7,9},{8,10},{9,11},{10,... | collective-permute-start | bytes 1769480 | tf_op jit(solution)/shard_map/ppermute | solution.py:19
  348.2 50.2 %collective-permute-start.16 = (f32[128,1152]{0,1:T(8,128)}, f32[128,1152]{0,1:T(8,128)}, u32[]{:S(2)}, u32[]{:S(2)}) collective-permute-start(f32[128,1152]{0,1:T(8,128)} %bitcast.101), channel_id=1, source_target_pairs={{3,0},{4,1},{5,2},{6,3},{7,4},{8,5},{9,6},{10,7},{11,8},{12,9},{13... | collective-permute-start | bytes 1769480 | tf_op jit(solution)/shard_map/ppermute | solution.py:19
  349.5 48.9 %collective-permute-start.17 = (f32[128,1152]{0,1:T(8,128)}, f32[128,1152]{0,1:T(8,128)}, u32[]{:S(2)}, u32[]{:S(2)}) collective-permute-start(f32[128,1152]{0,1:T(8,128)} %bitcast.103), channel_id=1, source_target_pairs={{0,3},{1,4},{2,5},{3,6},{4,7},{5,8},{6,9},{7,10},{8,11},{9,12},{10... | collective-permute-start | bytes 1769480 | tf_op jit(solution)/shard_map/ppermute | solution.py:19
  (32 other events, 466.0 us)
Sparse Core Ops, SparseCore 0:
  335.7 57.8 all-reduce.3
where the time goes:
time: 414 us; the launch traced here: 409 us
  starting transfers between devices  157 us (38%)
  blocking collectives  99.9 us (24%)
  local copies, waits for them, and re-layouts  42.6 us (10%)
  waiting for transfers between devices  41 us (10%)
  matrix products  34.7 us (8%)
  between operations  19.1 us (5%)
  other arithmetic  14.6 us (4%)
    ppermute x24, starting transfers between devices, shifted(): return lax.ppermute(block, axis, route)  105 us
    unnamed x1, blocking collectives  99.9 us
    unnamed x8, starting transfers between devices  51.6 us
    psum x1, waiting for transfers between devices, body(): weight_sum = lax.psum(weight_share, 'dp')  37.5 us
    unnamed x50, local copies, waits for them, and re-layouts  25.9 us
    broadcast_in_dim x16, local copies, waits for them, and re-layouts, body(): head_zeros = jnp.zeros((tok_rows, HEADS, HEAD_DIM), jnp.float32)  12.3 us
  transfers between devices with their start and end apart: 33, of which 3 were waited for; matrix products, arithmetic and copies ran while one was open for 19% of the time, Pallas kernels for 0%

commit v1 on v0

v1 whole, which is shorter than its diff:
```python
import functools

import jax
import jax.numpy as jnp
from jax import lax
from jax.experimental import pallas as pl
from jax.experimental.pallas import tpu as pltpu
from jax.sharding import PartitionSpec as P

NX, NZ = 4, 8
NY, NCORE = 4, 2
NDP = NY * NCORE
BLK = 128
HEADS, HD = 16, 72
HPD = HEADS // NX
FEAT = HPD * HD
D = HEADS * HD
REACH = 3
SLOTS = NX + 2 * REACH
NIMG = 20
TOKENS = 4096
ALL_TOK = 32768
SCALE = HD ** -0.5
NEG = -1e30
PADW = 80
CHUNK = 640
CSTEP = 512
NRED = 5
ROWS = D // (NX * NZ)

F32, BF16 = jnp.float32, jnp.bfloat16
MESH = pl.DeviceIdType.MESH
VM = pl.BlockSpec(memory_space=pltpu.VMEM)


def place():
    dp, seq = lax.axis_index("dp"), lax.axis_index("seq")
    return dp, lax.div(seq, NX), lax.rem(seq, NX)


def remote(src, dst, send, recv, device):
    return pltpu.make_async_remote_copy(
        src_ref=src, dst_ref=dst, send_sem=send, recv_sem=recv, device_id=device, device_id_type=MESH
    )


def hello(barrier, device):
    pl.semaphore_signal(barrier, inc=1, device_id=device, device_id_type=MESH)


def dot_nn(a, b):
    return lax.dot_general(a, b, (((1,), (0,)), ((), ())), preferred_element_type=F32)


def dot_nt(a, b):
    return lax.dot_general(a, b, (((1,), (1,)), ((), ())), preferred_element_type=F32)


def gather_kernel(
    q_ref, k_ref, v_ref, dy_ref, w_ref,
    qt_out, kt_out, vt_out, kr_out, vr_out, dt_out, dy_out,
    ksend, vsend, qsend, kwin, vwin, qwin, wbuf,
    x_send, x_recv, z_send, z_recv, w_sem,
):
    dp, z, x = place()
    up, down = lax.rem(z + 1, NZ), lax.rem(z + NZ - 1, NZ)
    barrier = pltpu.get_barrier_semaphore()
    order = (1, 3, 2)

    def xdev(o):
        return (dp, NX * z + lax.rem(x + o, NX))

    for o in order:
        hello(barrier, xdev(o))
    for zz in (up, down):
        hello(barrier, (dp, NX * zz + x))
    w_copy = pltpu.make_async_copy(w_ref.at[pl.ds(pl.multiple_of(FEAT * x, 32), FEAT)], wbuf, w_sem)
    w_copy.start()

    def turn(src, dst):
        for i in range(D // BLK):
            tile = src[0, :, i * BLK : (i + 1) * BLK].astype(F32)
            dst[i * BLK : (i + 1) * BLK, :] = tile.T.astype(BF16)

    def part(ref, xp):
        return ref.at[pl.ds(pl.multiple_of(FEAT * xp, 32), FEAT)]

    def x_copy(t, o, src, win, base):
        xp = lax.rem(x + o, NX)
        return remote(
            part(src, xp), win.at[base + x], x_send.at[t, o], x_recv.at[t, NX - o], xdev(o)
        )

    def x_wait(t, o, src, win, base):
        xp = lax.rem(x + o, NX)
        remote(part(src, xp), win.at[base + xp], x_send.at[t, o], x_recv.at[t, o], xdev(o)).wait_recv()

    def dy_copy(o):
        return remote(dy_ref.at[0], dy_out.at[x], x_send.at[3, o], x_recv.at[3, NX - o], xdev(o))

    turn(k_ref, ksend)
    pl.semaphore_wait(barrier, 5)
    for o in order:
        x_copy(0, o, ksend, kwin, REACH).start()
    turn(v_ref, vsend)
    for o in order:
        x_copy(1, o, vsend, vwin, REACH).start()
    turn(q_ref, qsend)
    for o in order:
        x_copy(2, o, qsend, qwin, 0).start()
    for o in order:
        dy_copy(o).start()
    mine = pl.ds(pl.multiple_of(FEAT * x, 32), FEAT)
    kwin[REACH + x] = ksend[mine, :]
    vwin[REACH + x] = vsend[mine, :]
    qwin[x] = qsend[mine, :]
    dy_out[x] = dy_ref[0]

    def z_up(t, xp, win):
        slot = xp + NX + REACH
        return remote(
            win.at[REACH + xp], win.at[slot], z_send.at[t, 0, xp], z_recv.at[t, 1, xp], (dp, NX * down + x)
        )

    def z_down(t, xp, win):
        slot = xp - 1
        return remote(
            win.at[REACH + xp], win.at[slot], z_send.at[t, 1, xp], z_recv.at[t, 0, xp], (dp, NX * up + x)
        )

    for t, src, win in ((0, ksend, kwin), (1, vsend, vwin)):
        for o in (0, 1, 3, 2):
            xp = lax.rem(x + o, NX)
            if o:
                x_wait(t, o, src, win, REACH)

            @pl.when(xp <= REACH - 1)
            def _():
                z_up(t, xp, win).start()

            @pl.when(xp >= 1)
            def _():
                z_down(t, xp, win).start()

    def unpack(win, slot, t_out, r_out):
        val = win[slot].astype(F32)
        for h in range(HPD):
            piece = val[h * HD : (h + 1) * HD]
            t_out[h, slot] = piece.astype(BF16)
            if r_out is not None:
                r_out[h, slot] = piece.T.astype(BF16)

    def unpack_kv(slot, carry):
        unpack(kwin, slot, kt_out, kr_out)
        unpack(vwin, slot, vt_out, vr_out)
        return carry

    lax.fori_loop(REACH, REACH + NX, unpack_kv, 0)
    for o in order:
        x_wait(2, o, qsend, qwin, 0)

    def unpack_q(slot, carry):
        unpack(qwin, slot, qt_out, None)
        return carry

    lax.fori_loop(0, NX, unpack_q, 0)

    for t, win in ((0, kwin), (1, vwin)):
        for xp in range(REACH):
            remote(
                win.at[REACH + xp], win.at[xp + NX + REACH], z_send.at[t, 0, xp], z_recv.at[t, 1, xp],
                (dp, NX * down + x),
            ).wait_recv()
            remote(
                win.at[REACH + xp + 1], win.at[xp], z_send.at[t, 1, xp + 1], z_recv.at[t, 0, xp + 1],
                (dp, NX * up + x),
            ).wait_recv()
    lax.fori_loop(0, REACH, unpack_kv, 0)
    lax.fori_loop(REACH + NX, SLOTS, unpack_kv, 0)

    w_copy.wait()
    for o in (0, 1, 3, 2):
        xp = lax.rem(x + o, NX)
        if o:
            remote(dy_ref.at[0], dy_out.at[xp], x_send.at[3, o], x_recv.at[3, o], xdev(o)).wait_recv()
        d_blk = dot_nt(wbuf[...], dy_out[xp])
        for h in range(HPD):
            dt_out[h, xp] = d_blk[h * HD : (h + 1) * HD].astype(BF16)

    for o in order:
        x_copy(0, o, ksend, kwin, REACH).wait_send()
        x_copy(1, o, vsend, vwin, REACH).wait_send()
        x_copy(2, o, qsend, qwin, 0).wait_send()
        dy_copy(o).wait_send()
    for t, win in ((0, kwin), (1, vwin)):
        for xp in range(REACH):
            z_up(t, xp, win).wait_send()
            z_down(t, xp + 1, win).wait_send()


def gather(queries, keys, values, out_grad, out_weight):
    heads_t = lambda n: jax.ShapeDtypeStruct((HPD, n, HD, BLK), BF16)
    heads_r = lambda n: jax.ShapeDtypeStruct((HPD, n, BLK, HD), BF16)
    dma = pltpu.SemaphoreType.DMA
    return pl.pallas_call(
        gather_kernel,
        out_shape=(
            heads_t(NX), heads_t(SLOTS), heads_t(SLOTS), heads_r(SLOTS), heads_r(SLOTS), heads_t(NX),
            jax.ShapeDtypeStruct((NX, BLK, D), BF16),
        ),
        in_specs=[VM] * 4 + [pl.BlockSpec(memory_space=pl.ANY)],
        out_specs=(VM,) * 7,
        scratch_shapes=[
            pltpu.VMEM((D, BLK), BF16),
            pltpu.VMEM((D, BLK), BF16),
            pltpu.VMEM((D, BLK), BF16),
            pltpu.VMEM((SLOTS, FEAT, BLK), BF16),
            pltpu.VMEM((SLOTS, FEAT, BLK), BF16),
            pltpu.VMEM((NX, FEAT, BLK), BF16),
            pltpu.VMEM((FEAT, D), BF16),
            dma((4, NX)),
            dma((4, NX)),
            dma((2, 2, NX)),
            dma((2, 2, NX)),
            dma,
        ],
        compiler_params=pltpu.CompilerParams(
            collective_id=0, has_side_effects=True, vmem_limit_bytes=40 * 2**20
        ),
        name="gather_heads",
    )(queries, keys, values, out_grad, out_weight)


def attend_kernel(
    len_ref, qt_ref, kt_ref, vt_ref, kr_ref, vr_ref, dt_ref, dy_ref,
    dq_out, dk_own, dv_own, dk_halo, dv_halo, wp_out,
    s_scr, p_scr, dq_acc, dk_acc, dv_acc, att_scr,
):
    z = lax.div(lax.axis_index("seq"), NX)
    first = (NX * z - REACH) * BLK
    dk_acc[...] = jnp.zeros_like(dk_acc)
    dv_acc[...] = jnp.zeros_like(dv_acc)

    ends = []
    total = jnp.int32(0)
    for i in range(NIMG):
        total = total + len_ref[0, i]
        ends.append(total)

    def bounds(pos):
        lo = jnp.zeros_like(pos)
        hi = jnp.full_like(pos, TOKENS)
        for e in ends:
            lo = jnp.where(e <= pos, e, lo)
        for e in reversed(ends):
            hi = jnp.where(e > pos, e, hi)
        return lo, hi

    def block(j, carry):
        base = (NX * z + j) * BLK
        lo_tok, _ = bounds(base)
        _, hi_tok = bounds(base + BLK - 1)
        k_lo = lax.div(lo_tok - first, BLK)
        k_hi = lax.div(hi_tok - first + BLK - 1, BLK)
        q_pos = base + lax.broadcasted_iota(jnp.int32, (8, BLK), 1)
        q_lo, q_hi = bounds(q_pos)
        q_lo, q_hi = q_lo[0:1], q_hi[0:1]
        rows = lax.broadcasted_iota(jnp.int32, (BLK, BLK), 0)

        def scores(kb, top):
            offset = first + kb * BLK
            keep = jnp.logical_and(rows >= q_lo - offset, rows < q_hi - offset)
            tops = []
            for h in range(HPD):
                s = dot_nn(kr_ref[h, kb], qt_ref[h, j]) * SCALE
                s = jnp.where(keep, s, NEG)
                s_scr[h, kb] = s
                tops.append(jnp.maximum(top[h], jnp.max(s, axis=0, keepdims=True)))
            return tuple(tops)

        top = lax.fori_loop(k_lo, k_hi, scores, (jnp.full((1, BLK), NEG, F32),) * HPD)

        def exps(kb, tot):
            out = []
            for h in range(HPD):
                e = jnp.exp(s_scr[h, kb] - top[h])
                s_scr[h, kb] = e
                out.append(tot[h] + jnp.sum(e, axis=0, keepdims=True))
            return tuple(out)

        norm = lax.fori_loop(k_lo, k_hi, exps, (jnp.zeros((1, BLK), F32),) * HPD)
        inv = [1.0 / n for n in norm]

        def mix(kb, acc):
            out = []
            for h in range(HPD):
                p = (s_scr[h, kb] * inv[h]).astype(BF16)
                p_scr[h, kb] = p
                out.append(acc[h] + dot_nn(vt_ref[h, kb], p))
            return tuple(out)

        mixed = lax.fori_loop(k_lo, k_hi, mix, (jnp.zeros((HD, BLK), F32),) * HPD)
        delta = []
        for h in range(HPD):
            att = mixed[h].astype(BF16)
            att_scr[h, j] = att
            delta.append(
                jnp.sum(dt_ref[h, j].astype(F32) * att.astype(F32), axis=0, keepdims=True)
            )

        def grads(kb, acc):
            out = []
            for h in range(HPD):
                feats = pl.ds(h * HD, HD)
                p = p_scr[h, kb]
                dp = dot_nn(vr_ref[h, kb], dt_ref[h, j])
                ds = (SCALE * p.astype(F32) * (dp - delta[h])).astype(BF16)
                out.append(acc[h] + dot_nn(kt_ref[h, kb], ds))
                dk_acc[kb, feats, :] += dot_nt(qt_ref[h, j], ds)
                dv_acc[kb, feats, :] += dot_nt(dt_ref[h, j], p)
            return tuple(out)

        dq = lax.fori_loop(k_lo, k_hi, grads, (jnp.zeros((HD, BLK), F32),) * HPD)
        for h in range(HPD):
            dq_acc[j, pl.ds(h * HD, HD), :] = dq[h]
        return carry

    lax.fori_loop(0, NX, block, 0)

    dq_out[...] = dq_acc[...].astype(BF16)
    for acc, own, halo in ((dk_acc, dk_own, dk_halo), (dv_acc, dv_own, dv_halo)):
        own[...] = acc[REACH : REACH + NX]
        halo[0:REACH] = acc[0:REACH].astype(BF16)
        halo[REACH:] = acc[REACH + NX :].astype(BF16)
    wp_out[...] = jnp.zeros_like(wp_out)
    for h in range(HPD):
        part = jnp.zeros((HD, D), F32)
        for j in range(NX):
            part = part + dot_nn(att_scr[h, j], dy_ref[j])
        wp_out[h, 0:HD, :] = part.astype(BF16)


def attend(lengths, qt, kt, vt, kr, vr, dt, dy):
    block = lambda n, dtype: jax.ShapeDtypeStruct((n, FEAT, BLK), dtype)
    return pl.pallas_call(
        attend_kernel,
        out_shape=(
            block(NX, BF16), block(NX, F32), block(NX, F32), block(2 * REACH, BF16),
            block(2 * REACH, BF16), jax.ShapeDtypeStruct((HPD, PADW, D), BF16),
        ),
        in_specs=[pl.BlockSpec(memory_space=pltpu.SMEM)] + [VM] * 7,
        out_specs=(VM,) * 6,
        scratch_shapes=[
            pltpu.VMEM((HPD, SLOTS, BLK, BLK), F32),
            pltpu.VMEM((HPD, SLOTS, BLK, BLK), BF16),
            pltpu.VMEM((NX, FEAT, BLK), F32),
            pltpu.VMEM((SLOTS, FEAT, BLK), F32),
            pltpu.VMEM((SLOTS, FEAT, BLK), F32),
            pltpu.VMEM((HPD, NX, HD, BLK), BF16),
        ],
        compiler_params=pltpu.CompilerParams(vmem_limit_bytes=48 * 2**20),
        name="attend",
    )(lengths, qt, kt, vt, kr, vr, dt, dy)


def return_kernel(
    dq_ref, dk_own, dv_own, dk_halo, dv_halo, wp_ref,
    gq_out, gk_out, gv_out, gw_out,
    rz_k, rz_v, t_k, t_v, rx_q, rx_k, rx_v, r1, s2, r2, tot, s3, r3,
    z_send, z_recv, x_send, x_recv, s1_send, s1_recv, s2_send, s2_recv, s3_send, s3_recv, l_sem,
):
    dp, z, x = place()
    seq = NX * z + x
    y, core = lax.div(dp, NCORE), lax.rem(dp, NCORE)
    up, down = lax.rem(z + 1, NZ), lax.rem(z + NZ - 1, NZ)
    barrier = pltpu.get_barrier_semaphore()
    reducer = z < NRED

    head = HPD * x + y
    owner = [2 * head, 2 * head + 1]
    my_head = lax.div(seq, 2)
    src_x, src_y = lax.div(my_head, HPD), lax.rem(my_head, HPD)
    half = lax.rem(seq, 2)

    def source(c, r):
        return (src_y * NCORE + c, NX * r + src_x)

    def is_source(c, r):
        return jnp.logical_and(
            jnp.logical_and(src_y * NCORE + c == dp, src_x == x), z == r
        )

    def is_me(t, d):
        return jnp.logical_and(owner[t] == seq, dp == d)

    for zz in (up, down):
        hello(barrier, (dp, NX * zz + x))
    for o in range(1, NX):
        hello(barrier, (dp, NX * z + lax.rem(x + o, NX)))
    for o in range(1, NDP):
        hello(barrier, (lax.rem(dp + o, NDP), seq))

    @pl.when(reducer)
    def _():
        for o in range(1, NZ):
            hello(barrier, (dp, NX * lax.rem(z + o, NZ) + x))

    for c in range(NCORE):
        for r in range(NRED):

            @pl.when(jnp.logical_not(is_source(c, r)))
            def _():
                hello(barrier, source(c, r))

    to_reducers = jnp.where(reducer, NRED - 1, NRED)
    mine_too = jnp.int32(0)
    for t in range(2):
        mine_too = mine_too + jnp.where(owner[t] == seq, 1, 0)
    to_owners = jnp.where(reducer, 2 * NDP - mine_too, 0)
    pl.semaphore_wait(barrier, 2 + NX - 1 + NDP - 1 + to_reducers + to_owners)

    def z_copy(t, halo, rz, side):
        zz = down if side == 0 else up
        return remote(
            halo.at[pl.ds(side * REACH, REACH)], rz.at[pl.ds(side * REACH, REACH)],
            z_send.at[t, side], z_recv.at[t, side], (dp, NX * zz + x),
        )

    kv = ((0, dk_halo, rz_k), (1, dv_halo, rz_v))
    for t, halo, rz in kv:
        for side in range(2):
            z_copy(t, halo, rz, side).start()

    def s1_copy(d):
        c = d % NCORE
        return remote(
            wp_ref.at[d // NCORE, :, pl.ds(CSTEP * c, CHUNK)], r1.at[dp],
            s1_send.at[d], s1_recv.at[dp], (jnp.int32(d), seq),
        )

    for d in range(NDP):

        @pl.when(d != dp)
        def _():
            s1_copy(d).start()

    def x_copy(t, src, rx, b):
        return remote(src.at[b], rx.at[x], x_send.at[t, b], x_recv.at[t, x], (dp, NX * z + b))

    def x_start(t, src, rx, b):
        @pl.when(b != x)
        def _():
            x_copy(t, src, rx, b).start()

        @pl.when(b == x)
        def _():
            rx[b] = src[b]

    def x_end(t, src, rx):
        for b in range(NX):

            @pl.when(b != x)
            def _():
                remote(
                    src.at[b], rx.at[b], x_send.at[t, b], x_recv.at[t, b], (dp, NX * z + b)
                ).wait_recv()

    def x_drain(t, src, rx):
        for b in range(NX):

            @pl.when(b != x)
            def _():
                x_copy(t, src, rx, b).wait_send()

    def give(rx, out):
        val = rx[...].astype(F32).reshape(D, BLK)
        for i in range(D // BLK):
            out[0, :, i * BLK : (i + 1) * BLK] = val[i * BLK : (i + 1) * BLK].T

    for b in range(NX):
        x_start(0, dq_ref, rx_q, b)

    for t, halo, rz, own, stage, rx in (
        (0, dk_halo, rz_k, dk_own, t_k, rx_k), (1, dv_halo, rz_v, dv_own, t_v, rx_v)
    ):
        for side in range(2):
            z_copy(t, halo, rz, side).wait_recv()
        for b in range(NX):
            val = own[b]
            if b >= 1:
                val = val + rz[b - 1].astype(F32)
            if b < REACH:
                val = val + rz[REACH + b].astype(F32)
            stage[b] = val.astype(BF16)
            x_start(1 + t, stage, rx, b)

    for d in range(NDP):

        @pl.when(d == dp)
        def _():
            r1[d] = wp_ref[d // NCORE, :, CSTEP * (d % NCORE) : CSTEP * (d % NCORE) + CHUNK]

    for d in range(NDP):

        @pl.when(d != dp)
        def _():
            remote(
                wp_ref.at[0, :, pl.ds(0, CHUNK)], r1.at[d], s1_send.at[d], s1_recv.at[d], (jnp.int32(d), seq)
            ).wait_recv()

    over_dp = r1[0].astype(F32)
    for d in range(1, NDP):
        over_dp = over_dp + r1[d].astype(F32)
    for r in range(NRED):
        s2[r] = over_dp[:, r * BLK : (r + 1) * BLK].astype(BF16)

    def s2_copy(r):
        return remote(s2.at[r], r2.at[z], s2_send.at[r], s2_recv.at[z], (dp, NX * r + x))

    for r in range(NRED):

        @pl.when(r != z)
        def _():
            s2_copy(r).start()

        @pl.when(r == z)
        def _():
            r2[r] = s2[r]

    x_end(0, dq_ref, rx_q)
    give(rx_q, gq_out)

    def s3_copy(t, d):
        return remote(
            s3.at[t], r3.at[core, z], s3_send.at[t, d], s3_recv.at[core, z], (jnp.int32(d), owner[t])
        )

    def s3_local(t):
        return pltpu.make_async_copy(s3.at[t], r3.at[core, z], l_sem)

    @pl.when(reducer)
    def _():
        for r in range(NZ):

            @pl.when(r != z)
            def _():
                remote(s2.at[0], r2.at[r], s2_send.at[0], s2_recv.at[r], (dp, NX * r + x)).wait_recv()

        over_z = r2[0].astype(F32)
        for r in range(1, NZ):
            over_z = over_z + r2[r].astype(F32)
        tot[...] = over_z * (ALL_TOK ** -0.5)
        s3[0] = tot[0:40, :]
        s3[1] = tot[ROWS : ROWS + 40, :]
        for t in range(2):
            for d in range(NDP):

                @pl.when(jnp.logical_not(is_me(t, d)))
                def _():
                    s3_copy(t, d).start()

                @pl.when(is_me(t, d))
                def _():
                    s3_local(t).start()

    x_end(1, t_k, rx_k)
    give(rx_k, gk_out)
    x_end(2, t_v, rx_v)
    give(rx_v, gv_out)

    for c in range(NCORE):
        for r in range(NRED):

            @pl.when(is_source(c, r))
            def _():
                pltpu.make_async_copy(s3.at[0], r3.at[c, r], l_sem).wait()

            @pl.when(jnp.logical_not(is_source(c, r)))
            def _():
                remote(
                    s3.at[0], r3.at[c, r], s3_send.at[0, 0], s3_recv.at[c, r], source(c, r)
                ).wait_recv()

            gw_out[:, c * CSTEP + r * BLK : c * CSTEP + (r + 1) * BLK] = r3[c, r, 0:ROWS, :]

    for t, halo, rz in kv:
        for side in range(2):
            z_copy(t, halo, rz, side).wait_send()
    for d in range(NDP):

        @pl.when(d != dp)
        def _():
            s1_copy(d).wait_send()

    x_drain(0, dq_ref, rx_q)
    x_drain(1, t_k, rx_k)
    x_drain(2, t_v, rx_v)
    for r in range(NRED):

        @pl.when(r != z)
        def _():
            s2_copy(r).wait_send()

    @pl.when(reducer)
    def _():
        for t in range(2):
            for d in range(NDP):

                @pl.when(jnp.logical_not(is_me(t, d)))
                def _():
                    s3_copy(t, d).wait_send()


def give_back(dq, dk_own, dv_own, dk_halo, dv_halo, wp):
    dma = pltpu.SemaphoreType.DMA
    grad = jax.ShapeDtypeStruct((1, BLK, D), F32)
    blocks = lambda n: pltpu.VMEM((n, FEAT, BLK), BF16)
    return pl.pallas_call(
        return_kernel,
        out_shape=(grad, grad, grad, jax.ShapeDtypeStruct((ROWS, D), F32)),
        in_specs=[VM] * 6,
        out_specs=(VM,) * 4,
        scratch_shapes=[
            blocks(2 * REACH), blocks(2 * REACH), blocks(NX), blocks(NX), blocks(NX), blocks(NX), blocks(NX),
            pltpu.VMEM((NDP, PADW, CHUNK), BF16),
            pltpu.VMEM((NRED, PADW, BLK), BF16),
            pltpu.VMEM((NZ, PADW, BLK), BF16),
            pltpu.VMEM((PADW, BLK), F32),
            pltpu.VMEM((2, 40, BLK), F32),
            pltpu.VMEM((NCORE, NRED, 40, BLK), F32),
            dma((2, 2)), dma((2, 2)), dma((3, NX)), dma((3, NX)),
            dma((NDP,)), dma((NDP,)), dma((NRED,)), dma((NZ,)), dma((2, NDP)), dma((NCORE, NRED)), dma,
        ],
        compiler_params=pltpu.CompilerParams(
            collective_id=1, has_side_effects=True, vmem_limit_bytes=40 * 2**20
        ),
        name="return_grads",
    )(dq, dk_own, dv_own, dk_halo, dv_halo, wp)


def body(queries, keys, values, out_weight, out_grad, lengths):
    qt, kt, vt, kr, vr, dt, dy = gather(queries, keys, values, out_grad, out_weight)
    grads = attend(lengths, qt, kt, vt, kr, vr, dt, dy)
    return give_back(*grads)


def solution(mesh):
    rows = P("dp", "seq", None)
    return jax.shard_map(
        body,
        mesh=mesh,
        in_specs=(rows, rows, rows, P(), rows, P("dp", None)),
        out_specs=(rows, rows, rows, P("seq", None)),
        check_vma=False,
    )
```

time: 414 us -> 120 us (0.29)
  the two profiles are of different devices: /device:TPU:8 before, /device:TPU:155 now
where the time goes in v1:
time: 120 us
  Pallas kernels  107 us (89%)
  local copies, waits for them, and re-layouts  11.9 us (10%)
    pallas_call x1, Pallas kernels, give_back(): pl.pallas_call(return_kernel, out_shape=(grad, grad, grad, jax.ShapeDtype...  55.4 us
    pallas_call x1, Pallas kernels, gather(): pl.pallas_call(gather_kernel, out_shape=(heads_t(NX), heads_t(SLOTS), hea...  26.3 us
    pallas_call x1, Pallas kernels, attend(): pl.pallas_call(attend_kernel, out_shape=(block(NX, BF16), block(NX, F32),...  25.8 us
    unnamed x22, local copies, waits for them, and re-layouts  11.9 us

profile of v1, /device:TPU:155, one launch (start us, length us, event | category | flops | bytes accessed | tf_op | source)
XLA Modules:
  0.0 119.9 jit_solution(5490503953115329225)
XLA Ops:
  0.6 0.0 copy-start
  0.6 1.7 %copy-done = bf16[1152,1152]{1,0:T(8,128)(2,1)S(1)} copy-done((bf16[1152,1152]{1,0:T(8,128)(2,1)S(1)}, bf16[1152,1152]{1,0:T(8,128)(2,1)}, u32[]{:S(2)}) %copy-start) | copy-done | bytes 2654232
  2.4 0.0 copy-start.4
  2.4 1.0 copy-done.4
  3.3 0.0 copy-start.5
  3.3 1.0 copy-done.5
  4.3 0.0 copy-start.6
  4.3 1.0 copy-done.6
  5.3 0.0 copy-start.7
  5.3 1.0 copy-done.7
  6.2 0.0 copy-start.8
  6.2 26.3 %gather_heads.1 = (bf16[4,4,72,128]{3,2,1,0:T(8,128)(2,1)S(1)}, bf16[4,10,72,128]{3,2,1,0:T(8,128)(2,1)S(1)}, bf16[4,10,72,128]{3,2,1,0:T(8,128)(2,1)S(1)}, bf16...) custom-call(bf16[1,128,1152]{2,1,0:T(8,128)(2,1)S(1)} %copy-done.4, ...), custom_call_target="tpu_custom_call" | custom-call | tf_op jit(solution)/shard_map/gather_heads/pallas_call | solution.py:205
  32.5 0.0 copy-start.1
  32.5 1.1 copy-done.1
  33.6 0.0 copy-start.2
  33.6 1.1 copy-done.2
  34.6 1.0 copy-done.3
  35.7 0.0 copy-done.8
  35.7 25.8 %attend.1 = (bf16[4,288,128]{2,1,0:T(8,128)(2,1)S(1)}, f32[4,288,128]{2,1,0:T(8,128)S(1)}, f32[4,288,128]{2,1,0:T(8,128)S(1)}, bf16[6,288,128]{2,1,0:T(8,128)(2,...) custom-call(s32[1,20]{1,0:T(1,128)S(1)} %copy-done.8, ...), custom_call_target="tpu_custom_call" | custom-call | tf_op jit(solution)/shard_map/attend/pallas_call | solution.py:345
  61.4 55.4 %return_grads.1 = (f32[1,128,1152]{2,1,0:T(8,128)S(1)}, f32[1,128,1152]{2,1,0:T(8,128)S(1)}, f32[1,128,1152]{2,1,0:T(8,128)S(1)}, f32[36,1152]{1,0:T(8,128)S(1)}) custom-call(bf16[4,288,128]{2,1,0:T(8,128)(2,1)S(1)} %get-tuple-element.24.dq_ref, f32[4,288,128]{2,1,0:T(8,128)S(1)} %get-tuple-element.25.dk_own, f32[4,288,128]{2,1,0:T(8,128)S(1)} %get-tuple-element.26.dv_own, ...), custom_call_target="tpu_custom_call" | custom-call | tf_op jit(solution)/shard_map/return_grads/pallas_call | solution.py:618
  116.8 0.8 copy.14
  117.6 0.8 copy.15
  118.4 0.8 copy.16
  119.3 0.7 copy.17
  (1 shorter events, 0.0 us)
Async XLA Ops:
  0.6 1.8 %copy-start = (bf16[1152,1152]{1,0:T(8,128)(2,1)S(1)}, bf16[1152,1152]{1,0:T(8,128)(2,1)}, u32[]{:S(2)}) copy-start(bf16[1152,1152]{1,0:T(8,128)(2,1)} %w_ref.1) | copy-start | bytes 7962628
  2.4 1.0 copy-start.4
  3.3 1.0 copy-start.5
  4.3 1.0 copy-start.6
  5.3 1.0 copy-start.7
  6.2 29.4 %copy-start.8 = (s32[1,20]{1,0:T(1,128)S(1)}, s32[1,20]{1,0:T(1,128)}, u32[]{:S(2)}) copy-start(s32[1,20]{1,0:T(1,128)} %len_ref.1) | copy-start | bytes 244
  32.5 1.1 copy-start.1
  33.6 1.1 copy-start.2
  34.6 1.0 copy-start.3

commit v2 on v0

v2 whole, which is shorter than its diff:
```python
import math

import jax
import jax.numpy as jnp
from jax import lax
from jax.experimental import pallas as pl
from jax.experimental.pallas import tpu as pltpu
from jax.sharding import PartitionSpec as P

NX, NZ = 4, 8
NY, NCORE = 4, 2
NDP = NY * NCORE
BLK = 128
HEADS, HD = 16, 72
HPD = HEADS // NX
FEAT = HPD * HD
D = HEADS * HD
REACH = 3
SLOTS = NX + 2 * REACH
WIDE = SLOTS * BLK
OWN = NX * BLK
NIMG = 20
TOKENS = 4096
ALL_TOK = 32768
SCALE = HD ** -0.5
LOG2E = math.log2(math.e)
NEG = -1e30
QG = 256
NG = OWN // QG
KG = QG + 2 * REACH * BLK
NCH = KG // BLK
PAIRS = HPD // 2
PF = 2 * HD
PADW = 80
CHUNK = 640
CSTEP = 512
NRED = 5
ROWS = D // (NX * NZ)
PADR = 48

F32, BF16 = jnp.float32, jnp.bfloat16
MESH = pl.DeviceIdType.MESH
VM = pl.BlockSpec(memory_space=pltpu.VMEM)
HB = pl.BlockSpec(memory_space=pltpu.HBM)


def remote(src, dst, send, recv, device):
    return pltpu.make_async_remote_copy(
        src_ref=src, dst_ref=dst, send_sem=send, recv_sem=recv, device_id=device, device_id_type=MESH
    )


def hello(barrier, device):
    pl.semaphore_signal(barrier, inc=1, device_id=device, device_id_type=MESH)


def dot_nn(a, b):
    return lax.dot_general(a, b, (((1,), (0,)), ((), ())), preferred_element_type=F32)


def dot_nt(a, b):
    return lax.dot_general(a, b, (((1,), (1,)), ((), ())), preferred_element_type=F32)


def main_kernel(
    len_ref, q_hbm, k_hbm, v_hbm, dy_hbm, w_hbm,
    rx_q, rx_k, rx_v, r3,
    kin, vin, qin, wbuf, dyw, ksend, vsend, qsend, kwin, vwin, qwin,
    qt, kt, vt, kr, vr, dt, s_scr, p_scr, ds_scr, att, dq_acc, dk_acc, dv_acc,
    dq_st, kh_st, vh_st, rz_k, rz_v, t_k, t_v,
    wp, r0, w1, r1, s2, r2, tot, s3,
    l_sem, x_send, x_recv, y_send, y_recv, f_send, f_recv, z_send, z_recv, g_send, g_recv,
    s0_send, s0_recv, s1_send, s1_recv, s2_send, s2_recv, s3_send, s3_recv, o_sem,
):
    dp, seq = lax.axis_index("dp"), lax.axis_index("seq")
    z, x = lax.div(seq, NX), lax.rem(seq, NX)
    y, core = lax.div(dp, NCORE), lax.rem(dp, NCORE)
    up, down = lax.rem(z + 1, NZ), lax.rem(z + NZ - 1, NZ)
    barrier = pltpu.get_barrier_semaphore()
    reducer = z < NRED
    order = (1, 3, 2)

    def xdev(o):
        return (dp, NX * z + lax.rem(x + o, NX))

    def zdev(zz):
        return (dp, NX * zz + x)

    def ydev(o):
        return (NCORE * lax.rem(y + o, NY) + core, seq)

    twin = (dp + 1 - 2 * core, seq)

    loads = [
        pltpu.make_async_copy(k_hbm.at[0], kin, l_sem.at[0]),
        pltpu.make_async_copy(v_hbm.at[0], vin, l_sem.at[1]),
        pltpu.make_async_copy(q_hbm.at[0], qin, l_sem.at[2]),
        pltpu.make_async_copy(dy_hbm.at[0], dyw.at[x], l_sem.at[3]),
        pltpu.make_async_copy(w_hbm.at[pl.ds(pl.multiple_of(FEAT * x, 32), FEAT)], wbuf, l_sem.at[4]),
    ]
    for copy in loads:
        copy.start()

    head = HPD * x + y
    owner = [2 * head, 2 * head + 1]
    my_head = lax.div(seq, 2)
    src_x, src_y = lax.div(my_head, HPD), lax.rem(my_head, HPD)

    def source(c, r):
        return (src_y * NCORE + c, NX * r + src_x)

    def is_source(c, r):
        return jnp.logical_and(jnp.logical_and(src_y * NCORE + c == dp, src_x == x), z == r)

    def is_me(t, d):
        return jnp.logical_and(owner[t] == seq, dp == d)

    for o in order:
        hello(barrier, xdev(o))
    for zz in (up, down):
        hello(barrier, zdev(zz))
    hello(barrier, twin)
    for o in order:
        hello(barrier, ydev(o))

    @pl.when(reducer)
    def _():
        for o in range(1, NZ):
            hello(barrier, zdev(lax.rem(z + o, NZ)))

    for c in range(NCORE):
        for r in range(NRED):

            @pl.when(jnp.logical_not(is_source(c, r)))
            def _():
                hello(barrier, source(c, r))

    to_reducers = jnp.where(reducer, NRED - 1, NRED)
    mine_too = jnp.int32(0)
    for t in range(2):
        mine_too = mine_too + jnp.where(owner[t] == seq, 1, 0)
    to_owners = jnp.where(reducer, 2 * NDP - mine_too, 0)

    def turn(src, dst):
        for i in range(D // BLK):
            tile = src[:, i * BLK : (i + 1) * BLK].astype(F32)
            dst[i * BLK : (i + 1) * BLK, :] = tile.T.astype(BF16)

    def part(ref, xp):
        return ref.at[pl.ds(pl.multiple_of(FEAT * xp, 32), FEAT)]

    def x_copy(t, o, src, win, base):
        xp = lax.rem(x + o, NX)
        return remote(part(src, xp), win.at[base + x], x_send.at[t, o], x_recv.at[t, NX - o], xdev(o))

    def x_wait(t, o, src, win, base):
        xp = lax.rem(x + o, NX)
        remote(part(src, xp), win.at[base + xp], x_send.at[t, o], x_recv.at[t, o], xdev(o)).wait_recv()

    def y_copy(o):
        return remote(dyw.at[x], dyw.at[x], y_send.at[o], y_recv.at[NX - o], xdev(o))

    def y_wait(o):
        xp = lax.rem(x + o, NX)
        remote(dyw.at[x], dyw.at[xp], y_send.at[o], y_recv.at[o], xdev(o)).wait_recv()

    def y_relay():
        xp = lax.rem(x + NX - RELAY, NX)
        return remote(dyw.at[xp], dyw.at[xp], y_send.at[2], y_recv.at[2], xdev(RELAY))

    mine = pl.ds(pl.multiple_of(FEAT * x, 32), FEAT)
    loads[0].wait()
    turn(kin, ksend)
    pl.semaphore_wait(barrier, 2 * (NX - 1) + 3 + to_reducers + to_owners)
    for o in order:
        x_copy(0, o, ksend, kwin, REACH).start()
    loads[1].wait()
    turn(vin, vsend)
    for o in order:
        x_copy(1, o, vsend, vwin, REACH).start()
    loads[2].wait()
    turn(qin, qsend)
    for o in order:
        x_copy(2, o, qsend, qwin, 0).start()
    loads[3].wait()
    for o in (NX - RELAY, RELAY)[::-1]:
        y_copy(o).start()
    kwin[REACH + x] = ksend[mine, :]
    vwin[REACH + x] = vsend[mine, :]
    qwin[x] = qsend[mine, :]

    def z_up(t, xp, win):
        return remote(
            win.at[REACH + xp], win.at[xp + NX + REACH], f_send.at[t, 0, xp], f_recv.at[t, 0, xp], zdev(down)
        )

    def z_down(t, xp, win):
        return remote(win.at[REACH + xp], win.at[xp - 1], f_send.at[t, 1, xp], f_recv.at[t, 1, xp], zdev(up))

    for t, src, win in ((0, ksend, kwin), (1, vsend, vwin)):
        for o in (0,) + order:
            xp = lax.rem(x + o, NX)
            if o:
                x_wait(t, o, src, win, REACH)

            @pl.when(xp < REACH)
            def _():
                z_up(t, xp, win).start()

            @pl.when(xp >= 1)
            def _():
                z_down(t, xp, win).start()

    def unpack(win, slot, t_out, r_out):
        val = win[slot].astype(F32)
        cols = pl.ds(pl.multiple_of(slot * BLK, BLK), BLK)
        for h in range(HPD):
            piece = val[h * HD : (h + 1) * HD]
            t_out[h, :, cols] = piece.astype(BF16)
            if r_out is not None:
                r_out[h, cols, :] = piece.T.astype(BF16)

    def unpack_kv(slot, carry):
        unpack(kwin, slot, kt, kr)
        unpack(vwin, slot, vt, vr)
        return carry

    def unpack_q(slot, carry):
        unpack(qwin, slot, qt, None)
        return carry

    lax.fori_loop(REACH, REACH + NX, unpack_kv, 0)
    for o in order:
        x_wait(2, o, qsend, qwin, 0)
    lax.fori_loop(0, NX, unpack_q, 0)
    for t, win in ((0, kwin), (1, vwin)):
        for xp in range(REACH):
            z_up(t, xp, win).wait_recv()
            z_down(t, xp + 1, win).wait_recv()
    lax.fori_loop(0, REACH, unpack_kv, 0)
    lax.fori_loop(REACH + NX, SLOTS, unpack_kv, 0)
    y_wait(NX - RELAY)
    y_relay().start()

    first = (NX * z - REACH) * BLK
    rows = lax.broadcasted_iota(jnp.int32, (BLK, QG), 0)
    ends = []
    total = jnp.int32(0)
    for i in range(NIMG):
        total = total + len_ref[0, i]
        ends.append(total)

    spans = []
    for g in range(NG):
        pos = NX * z * BLK + g * QG + lax.broadcasted_iota(jnp.int32, (8, QG), 1)
        lo = jnp.zeros_like(pos)
        hi = jnp.full_like(pos, TOKENS)
        for e in ends:
            lo = jnp.where(e <= pos, e, lo)
        for e in ends[::-1]:
            hi = jnp.where(e > pos, e, hi)
        spans.append((lo[0:1] - first - g * QG, hi[0:1] - first - g * QG))

    def forward(h, carry):
        for g in range(NG):
            lo, hi = spans[g]
            q_blk = qt[h, :, g * QG : (g + 1) * QG]
            top = jnp.full((1, QG), NEG, F32)
            for c in range(NCH):
                keys = slice(g * QG + c * BLK, g * QG + (c + 1) * BLK)
                s = dot_nn(kr[h, keys, :], q_blk)
                keep = jnp.logical_and(rows >= lo - c * BLK, rows < hi - c * BLK)
                s = jnp.where(keep, s, NEG)
                s_scr[g, c * BLK : (c + 1) * BLK, :] = s
                top = jnp.maximum(top, jnp.max(s, axis=0, keepdims=True))
            norm = jnp.zeros((1, QG), F32)
            for c in range(NCH):
                e = jnp.exp2((s_scr[g, c * BLK : (c + 1) * BLK, :] - top) * (SCALE * LOG2E))
                s_scr[g, c * BLK : (c + 1) * BLK, :] = e
                norm = norm + jnp.sum(e, axis=0, keepdims=True)
            inv = 1.0 / norm
            for c in range(NCH):
                p_scr[g, h, c * BLK : (c + 1) * BLK, :] = (
                    s_scr[g, c * BLK : (c + 1) * BLK, :] * inv
                ).astype(BF16)
            mixed = dot_nn(vt[h, :, g * QG : g * QG + KG], p_scr[g, h])
            att[h, :, g * QG : (g + 1) * QG] = mixed.astype(BF16)
        return carry

    lax.fori_loop(0, HPD, forward, 0)

    loads[4].wait()
    y_wait(RELAY)
    xp2 = lax.rem(x + 2, NX)
    remote(dyw.at[xp2], dyw.at[xp2], y_send.at[2], y_recv.at[2], xdev(RELAY)).wait_recv()
    for b in range(NX):
        d_blk = dot_nt(wbuf[...], dyw[b])
        for h in range(HPD):
            dt[h, :, b * BLK : (b + 1) * BLK] = d_blk[h * HD : (h + 1) * HD].astype(BF16)
    wp[...] = jnp.zeros_like(wp)
    dy_all = dyw[...].reshape(OWN, D)
    for h in range(HPD):
        wp[h, 0:HD, :] = dot_nn(att[h], dy_all).astype(BF16)

    far = pl.ds(pl.multiple_of(CSTEP * (1 - core), BLK), CHUNK)
    near = pl.ds(pl.multiple_of(CSTEP * core, BLK), CHUNK)
    s0_copy = remote(wp.at[:, :, far], r0, s0_send, s0_recv, twin)
    s0_copy.start()

    def s1_copy(o):
        return remote(
            w1.at[lax.rem(y + o, NY)], r1.at[NY - o], s1_send.at[o], s1_recv.at[NY - o], ydev(o)
        )

    def s1_begin():
        s0_copy.wait_recv()
        for h in range(HPD):
            w1[h] = (wp[h, :, near].astype(F32) + r0[h].astype(F32)).astype(BF16)
        for o in order:
            s1_copy(o).start()

    def s2_copy(r):
        return remote(s2.at[r], r2.at[z], s2_send.at[r], s2_recv.at[z], (dp, NX * r + x))

    def s2_begin():
        over_dp = w1[y].astype(F32)
        for o in order:
            remote(w1.at[0], r1.at[o], s1_send.at[o], s1_recv.at[o], ydev(o)).wait_recv()
            over_dp = over_dp + r1[o].astype(F32)
        for r in range(NRED):
            s2[r] = over_dp[:, r * BLK : (r + 1) * BLK].astype(BF16)
        for r in range(NRED):

            @pl.when(r != z)
            def _():
                s2_copy(r).start()

            @pl.when(r == z)
            def _():
                r2[r] = s2[r]

    def s3_copy(t, d):
        return remote(
            s3.at[t], r3.at[core, z], s3_send.at[t, d], s3_recv.at[core, z], (jnp.int32(d), owner[t])
        )

    def s3_begin():
        @pl.when(reducer)
        def _():
            for r in range(NZ):

                @pl.when(r != z)
                def _():
                    remote(s2.at[0], r2.at[r], s2_send.at[0], s2_recv.at[r], (dp, NX * r + x)).wait_recv()

            over_z = r2[0].astype(F32)
            for r in range(1, NZ):
                over_z = over_z + r2[r].astype(F32)
            tot[0:PADW, :] = over_z * (ALL_TOK ** -0.5)
            tot[PADW:, :] = jnp.zeros((8, BLK), F32)
            for t in range(2):
                s3[t] = tot[t * ROWS : t * ROWS + PADR, :].astype(BF16)
            for t in range(2):
                for d in range(NDP):

                    @pl.when(jnp.logical_not(is_me(t, d)))
                    def _():
                        s3_copy(t, d).start()

                    @pl.when(is_me(t, d))
                    def _():
                        pltpu.make_async_copy(s3.at[t], r3.at[core, z], o_sem).start()

    def backward(h, i, pair):
        feats = slice(i * HD, (i + 1) * HD)
        for g in range(NG):
            cols = slice(g * QG, (g + 1) * QG)
            q_blk, d_blk, p_all = qt[h, :, cols], dt[h, :, cols], p_scr[g, h]
            delta = jnp.sum(d_blk.astype(F32) * att[h, :, cols].astype(F32), axis=0, keepdims=True)
            for c in range(NCH):
                keys = slice(g * QG + c * BLK, g * QG + (c + 1) * BLK)
                dp_c = dot_nn(vr[h, keys, :], d_blk)
                p = p_scr[g, h, c * BLK : (c + 1) * BLK, :].astype(F32)
                ds_scr[g, c * BLK : (c + 1) * BLK, :] = (SCALE * p * (dp_c - delta)).astype(BF16)
            ds = ds_scr[g]
            dq_acc[pair, feats, cols] = dot_nn(kt[h, :, g * QG : g * QG + KG], ds)
            for acc, left, right in ((dk_acc, q_blk, ds), (dv_acc, d_blk, p_all)):
                add = dot_nt(left, right)
                if g == 0:
                    acc[pair, feats, 0:KG] = add
                else:
                    old = g * QG + KG - QG
                    acc[pair, feats, g * QG : old] += add[:, 0 : KG - QG]
                    acc[pair, feats, old : old + QG] = add[:, KG - QG :]

    def z_copy(t, p, side):
        stage, rz = ((kh_st, rz_k), (vh_st, rz_v))[t]
        zz = down if side == 0 else up
        slots = pl.ds(side * REACH, REACH)
        return remote(
            stage.at[p, slots], rz.at[p, slots], z_send.at[t, p, side], z_recv.at[t, p, side], zdev(zz)
        )

    returns = ((dq_st, rx_q), (t_k, rx_k), (t_v, rx_v))

    def g_copy(t, p, b):
        stage, rx = returns[t]
        return remote(
            stage.at[p, b], rx.at[x, pl.ds(PF * p, PF)], g_send.at[t, p, b], g_recv.at[t, p, x], (dp, NX * z + b)
        )

    def g_start(t, p, b):
        stage, rx = returns[t]

        @pl.when(b != x)
        def _():
            g_copy(t, p, b).start()

        @pl.when(b == x)
        def _():
            rx[b, PF * p : PF * (p + 1), :] = stage[p, b]

    def g_wait(t, p):
        stage, rx = returns[t]
        for b in range(NX):

            @pl.when(b != x)
            def _():
                remote(
                    stage.at[p, b], rx.at[b, pl.ds(PF * p, PF)], g_send.at[t, p, b], g_recv.at[t, p, b],
                    (dp, NX * z + b),
                ).wait_recv()

    def halo_send(p):
        for t, acc, stage in ((0, dk_acc, kh_st), (1, dv_acc, vh_st)):
            for side in range(2):
                for i in range(REACH):
                    slot = i + side * (NX + REACH)
                    stage[p, side * REACH + i] = acc[p, :, slot * BLK : (slot + 1) * BLK].astype(BF16)
                z_copy(t, p, side).start()
        for b in range(NX):
            dq_st[p, b] = dq_acc[p, :, b * BLK : (b + 1) * BLK].astype(BF16)
            g_start(0, p, b)

    def halo_add(p):
        for t, acc, rz in ((0, dk_acc, rz_k), (1, dv_acc, rz_v)):
            for side in range(2):
                z_copy(t, p, side).wait_recv()
            stage = returns[1 + t][0]
            for b in range(NX):
                val = acc[p, :, (REACH + b) * BLK : (REACH + b + 1) * BLK]
                if b >= 1:
                    val = val + rz[p, b - 1].astype(F32)
                if b < REACH:
                    val = val + rz[p, REACH + b].astype(F32)
                stage[p, b] = val.astype(BF16)
                g_start(1 + t, p, b)

    backward(0, 0, 0)
    s1_begin()
    backward(1, 1, 0)
    halo_send(0)
    backward(2, 0, 1)
    backward(3, 1, 1)
    halo_send(1)
    s2_begin()
    halo_add(0)
    s3_begin()
    halo_add(1)

    for c in range(NCORE):
        for r in range(NRED):

            @pl.when(is_source(c, r))
            def _():
                pltpu.make_async_copy(s3.at[0], r3.at[c, r], o_sem).wait()

            @pl.when(jnp.logical_not(is_source(c, r)))
            def _():
                remote(s3.at[0], r3.at[c, r], s3_send.at[0, 0], s3_recv.at[c, r], source(c, r)).wait_recv()

    for t in range(3):
        for p in range(PAIRS):
            g_wait(t, p)
    for o in order:
        x_copy(0, o, ksend, kwin, REACH).wait_send()
        x_copy(1, o, vsend, vwin, REACH).wait_send()
        x_copy(2, o, qsend, qwin, 0).wait_send()
    y_copy(RELAY).wait_send()
    y_copy(NX - RELAY).wait_send()
    y_relay().wait_send()
    for t, win in ((0, kwin), (1, vwin)):
        for xp in range(REACH):
            z_up(t, xp, win).wait_send()
            z_down(t, xp + 1, win).wait_send()
    for t in range(2):
        for p in range(PAIRS):
            for side in range(2):
                z_copy(t, p, side).wait_send()
    for t in range(3):
        for p in range(PAIRS):
            for b in range(NX):

                @pl.when(b != x)
                def _():
                    g_copy(t, p, b).wait_send()

    s0_copy.wait_send()
    for o in order:
        s1_copy(o).wait_send()
    for r in range(NRED):

        @pl.when(r != z)
        def _():
            s2_copy(r).wait_send()

    @pl.when(reducer)
    def _():
        for t in range(2):
            for d in range(NDP):

                @pl.when(jnp.logical_not(is_me(t, d)))
                def _():
                    s3_copy(t, d).wait_send()


RELAY = NX - 1


def main_call(lengths, queries, keys, values, out_grad, out_weight):
    dma = pltpu.SemaphoreType.DMA
    b16 = lambda *shape: pltpu.VMEM(shape, BF16)
    f32 = lambda *shape: pltpu.VMEM(shape, F32)
    back = jax.ShapeDtypeStruct((NX, FEAT, BLK), BF16)
    return pl.pallas_call(
        main_kernel,
        out_shape=(back, back, back, jax.ShapeDtypeStruct((NCORE, NRED, PADR, BLK), BF16)),
        in_specs=[pl.BlockSpec(memory_space=pltpu.SMEM)] + [HB] * 5,
        out_specs=(VM,) * 4,
        scratch_shapes=[
            b16(BLK, D), b16(BLK, D), b16(BLK, D), b16(FEAT, D), b16(NX, BLK, D),
            b16(D, BLK), b16(D, BLK), b16(D, BLK),
            b16(SLOTS, FEAT, BLK), b16(SLOTS, FEAT, BLK), b16(NX, FEAT, BLK),
            b16(HPD, HD, OWN), b16(HPD, HD, WIDE), b16(HPD, HD, WIDE), b16(HPD, WIDE, HD), b16(HPD, WIDE, HD),
            b16(HPD, HD, OWN),
            f32(NG, KG, QG), b16(NG, HPD, KG, QG), b16(NG, KG, QG), b16(HPD, HD, OWN),
            f32(PAIRS, PF, OWN), f32(PAIRS, PF, WIDE), f32(PAIRS, PF, WIDE),
            b16(PAIRS, NX, PF, BLK), b16(PAIRS, 2 * REACH, PF, BLK), b16(PAIRS, 2 * REACH, PF, BLK),
            b16(PAIRS, 2 * REACH, PF, BLK), b16(PAIRS, 2 * REACH, PF, BLK),
            b16(PAIRS, NX, PF, BLK), b16(PAIRS, NX, PF, BLK),
            b16(HPD, PADW, D), b16(HPD, PADW, CHUNK), b16(HPD, PADW, CHUNK), b16(NY, PADW, CHUNK),
            b16(NRED, PADW, BLK), b16(NZ, PADW, BLK), f32(PADW + 8, BLK), b16(2, PADR, BLK),
            dma((5,)), dma((3, NX)), dma((3, NX)), dma((NX,)), dma((NX,)), dma((2, 2, NX)), dma((2, 2, NX)),
            dma((2, PAIRS, 2)), dma((2, PAIRS, 2)), dma((3, PAIRS, NX)), dma((3, PAIRS, NX)),
            dma, dma, dma((NY,)), dma((NY,)), dma((NRED,)), dma((NZ,)), dma((2, NDP)), dma((NCORE, NRED)), dma,
        ],
        compiler_params=pltpu.CompilerParams(
            collective_id=0, has_side_effects=True, vmem_limit_bytes=52 * 2**20
        ),
        name="attention_backward",
    )(lengths, queries, keys, values, out_grad, out_weight)


PART = 3 * BLK


def finish_kernel(rq, rk, rv, rw, gq, gk, gv, gw):
    for src, dst in ((rq, gq), (rk, gk), (rv, gv)):
        for i in range(PART // BLK):
            tile = src[i * BLK : (i + 1) * BLK, :].astype(F32)
            dst[0, :, i * BLK : (i + 1) * BLK] = tile.T

    @pl.when(pl.program_id(0) == 0)
    def _():
        for c in range(NCORE):
            for r in range(NRED):
                col = c * CSTEP + r * BLK
                gw[:, col : col + BLK] = rw[c, r, 0:ROWS, :].astype(F32)


def finish(rq, rk, rv, rw):
    grad = jax.ShapeDtypeStruct((1, BLK, D), F32)
    wide = pl.BlockSpec((PART, BLK), lambda i: (i, 0))
    tall = pl.BlockSpec((1, BLK, PART), lambda i: (0, 0, i))
    return pl.pallas_call(
        finish_kernel,
        grid=(D // PART,),
        out_shape=(grad, grad, grad, jax.ShapeDtypeStruct((ROWS, D), F32)),
        in_specs=[wide] * 3 + [pl.BlockSpec((NCORE, NRED, PADR, BLK), lambda i: (0, 0, 0, 0))],
        out_specs=(tall, tall, tall, pl.BlockSpec((ROWS, D), lambda i: (0, 0))),
        name="outputs",
    )(*[r.reshape(D, BLK) for r in (rq, rk, rv)], rw)


def body(queries, keys, values, out_weight, out_grad, lengths):
    return finish(*main_call(lengths, queries, keys, values, out_grad, out_weight))


def solution(mesh):
    rows = P("dp", "seq", None)
    return jax.shard_map(
        body,
        mesh=mesh,
        in_specs=(rows, rows, rows, P(), rows, P("dp", None)),
        out_specs=(rows, rows, rows, P("seq", None)),
        check_vma=False,
    )
```

time: 414 us -> 84.8 us (0.20)
  the two profiles are of different devices: /device:TPU:8 before, /device:TPU:155 now
where the time goes in v2:
time: 84.8 us; the launch traced here: 84.5 us
  Pallas kernels  77.5 us (91%)
  local copies, waits for them, and re-layouts  6.33 us (7%)
    pallas_call x1, Pallas kernels, main_call(): pl.pallas_call(main_kernel, out_shape=(back, back, back, jax.ShapeDtypeSt...  73.8 us
    unnamed x16, local copies, waits for them, and re-layouts  6.33 us
    pallas_call x1, Pallas kernels, finish(): pl.pallas_call(finish_kernel, grid=(D // PART,), out_shape=(grad, grad, g...  3.67 us

profile of v2, /device:TPU:155, one launch (start us, length us, event | category | flops | bytes accessed | tf_op | source)
XLA Modules:
  0.0 84.5 jit_solution(1250653636671503806)
XLA Ops:
  0.6 0.0 copy-start
  0.6 1.0 %copy-done = bf16[1,128,1152]{2,1,0:T(8,128)(2,1)S(1)} copy-done((bf16[1,128,1152]{2,1,0:T(8,128)(2,1)S(1)}, bf16[1,128,1152]{2,1,0:T(8,128)(2,1)}, u32[]{:S(2)}) %copy-start) | copy-done | bytes 294936
  1.6 0.0 copy-start.1
  1.6 1.0 %copy-done.1 = bf16[1,128,1152]{2,1,0:T(8,128)(2,1)S(1)} copy-done((bf16[1,128,1152]{2,1,0:T(8,128)(2,1)S(1)}, bf16[1,128,1152]{2,1,0:T(8,128)(2,1)}, u32[]{:S(2)}) %copy-start.1) | copy-done | bytes 294936
  2.6 0.0 copy-start.2
  2.6 1.0 %copy-done.2 = bf16[1,128,1152]{2,1,0:T(8,128)(2,1)S(1)} copy-done((bf16[1,128,1152]{2,1,0:T(8,128)(2,1)S(1)}, bf16[1,128,1152]{2,1,0:T(8,128)(2,1)}, u32[]{:S(2)}) %copy-start.2) | copy-done | bytes 294936
  3.5 0.0 copy-start.7
  3.5 0.7 copy-done.7
  4.2 73.8 %attention_backward.1 = (bf16[4,288,128]{2,1,0:T(8,128)(2,1)S(1)}, bf16[4,288,128]{2,1,0:T(8,128)(2,1)S(1)}, bf16[4,288,128]{2,1,0:T(8,128)(2,1)S(1)}, bf16[2,5,48,128]{3,2,1,0:T(8,128)(2,1)S(1)}) custom-call(s32[1,20]{1,0:T(1,128)S(1)} %copy-done.7, bf16[1,128,1152]{2,1,0:T(8,128)(2,1)S(1)} %copy-done, bf16[1,128,1152]{2,1,0:T(8,128)(2,1)S(1)} %copy-done.1, ...), custom_call_target="tpu_custom_call" | custom-call | tf_op jit(solution)/shard_map/attention_backward/pallas_call | solution.py:535
  78.0 0.0 copy-start.3
  78.0 0.7 copy-done.3
  78.7 0.0 copy-start.4
  78.7 0.7 copy-done.4
  79.4 0.0 copy-start.5
  79.4 0.7 copy-done.5
  80.2 0.0 copy-start.6
  80.2 0.6 copy-done.6
  80.8 3.7 %outputs.1 = (f32[1,128,1152]{2,1,0:T(8,128)}, f32[1,128,1152]{2,1,0:T(8,128)}, f32[1,128,1152]{2,1,0:T(8,128)}, f32[36,1152]{1,0:T(8,128)}) custom-call(bf16[1152,128]{1,0:T(8,128)(2,1)} %bitcast.3, bf16[1152,128]{1,0:T(8,128)(2,1)} %bitcast.4, bf16[1152,128]{1,0:T(8,128)(2,1)} %bitcast.5, bf16[2,5,48,128]{3,2,1,0:T(8,128)(2,1)} %copy-done.6), custom_call_target="tpu_custom_call" | custom-call | tf_op jit(solution)/shard_map/outputs/pallas_call | solution.py:585
Async XLA Ops:
  0.6 1.0 %copy-start = (bf16[1,128,1152]{2,1,0:T(8,128)(2,1)S(1)}, bf16[1,128,1152]{2,1,0:T(8,128)(2,1)}, u32[]{:S(2)}) copy-start(bf16[1,128,1152]{2,1,0:T(8,128)(2,1)} %q_hbm.1) | copy-start | bytes 884740
  1.6 1.0 %copy-start.1 = (bf16[1,128,1152]{2,1,0:T(8,128)(2,1)S(1)}, bf16[1,128,1152]{2,1,0:T(8,128)(2,1)}, u32[]{:S(2)}) copy-start(bf16[1,128,1152]{2,1,0:T(8,128)(2,1)} %k_hbm.1) | copy-start | bytes 884740
  2.6 1.0 %copy-start.2 = (bf16[1,128,1152]{2,1,0:T(8,128)(2,1)S(1)}, bf16[1,128,1152]{2,1,0:T(8,128)(2,1)}, u32[]{:S(2)}) copy-start(bf16[1,128,1152]{2,1,0:T(8,128)(2,1)} %v_hbm.1) | copy-start | bytes 884740
  3.5 0.7 copy-start.7
  78.0 0.7 copy-start.3
  78.7 0.7 copy-start.4
  79.4 0.7 copy-start.5
  80.2 0.6 copy-start.6

commit v3 on v2

--- a/solution.py
+++ b/solution.py
@@ -68,9 +68,9 @@
     kin, vin, qin, wbuf, dyw, ksend, vsend, qsend, kwin, vwin, qwin,
     qt, kt, vt, kr, vr, dt, s_scr, p_scr, ds_scr, att, dq_acc, dk_acc, dv_acc,
     dq_st, kh_st, vh_st, rz_k, rz_v, t_k, t_v,
-    wp, r0, w1, r1, s2, r2, tot, s3,
+    wp, r0, w1, r1, s2, r2, tot, s3, h5,
     l_sem, x_send, x_recv, y_send, y_recv, f_send, f_recv, z_send, z_recv, g_send, g_recv,
-    s0_send, s0_recv, s1_send, s1_recv, s2_send, s2_recv, s3_send, s3_recv, o_sem,
+    s0_send, s0_recv, s1_send, s1_recv, s2_send, s2_recv, s3_send, s3_recv, s4_send, s4_recv, s5_send, s5_recv,
 ):
     dp, seq = lax.axis_index("dp"), lax.axis_index("seq")
     z, x = lax.div(seq, NX), lax.rem(seq, NX)
@@ -105,15 +105,10 @@
     owner = [2 * head, 2 * head + 1]
     my_head = lax.div(seq, 2)
     src_x, src_y = lax.div(my_head, HPD), lax.rem(my_head, HPD)
-
-    def source(c, r):
-        return (src_y * NCORE + c, NX * r + src_x)
-
-    def is_source(c, r):
-        return jnp.logical_and(jnp.logical_and(src_y * NCORE + c == dp, src_x == x), z == r)
-
-    def is_me(t, d):
-        return jnp.logical_and(owner[t] == seq, dp == d)
+    collector = src_y == y
+
+    def is_source(r):
+        return jnp.logical_and(src_x == x, z == r)
 
     for o in order:
         hello(barrier, xdev(o))
@@ -128,18 +123,17 @@
         for o in range(1, NZ):
             hello(barrier, zdev(lax.rem(z + o, NZ)))
 
-    for c in range(NCORE):
-        for r in range(NRED):
-
-            @pl.when(jnp.logical_not(is_source(c, r)))
-            def _():
-                hello(barrier, source(c, r))
+    for r in range(NRED):
+
+        @pl.when(jnp.logical_and(collector, jnp.logical_not(is_source(r))))
+        def _():
+            hello(barrier, (dp, NX * r + src_x))
 
     to_reducers = jnp.where(reducer, NRED - 1, NRED)
     mine_too = jnp.int32(0)
     for t in range(2):
         mine_too = mine_too + jnp.where(owner[t] == seq, 1, 0)
-    to_owners = jnp.where(reducer, 2 * NDP - mine_too, 0)
+    to_owners = jnp.where(reducer, 2 - mine_too, 0)
 
     def turn(src, dst):
         for i in range(D // BLK):
@@ -158,15 +152,19 @@
         remote(part(src, xp), win.at[base + xp], x_send.at[t, o], x_recv.at[t, o], xdev(o)).wait_recv()
 
     def y_copy(o):
-        return remote(dyw.at[x], dyw.at[x], y_send.at[o], y_recv.at[NX - o], xdev(o))
+        return remote(dyw.at[x], dyw.at[x], y_send.at[o // 2], y_recv.at[(NX - o) // 2], xdev(o))
 
     def y_wait(o):
         xp = lax.rem(x + o, NX)
-        remote(dyw.at[x], dyw.at[xp], y_send.at[o], y_recv.at[o], xdev(o)).wait_recv()
-
-    def y_relay():
-        xp = lax.rem(x + NX - RELAY, NX)
-        return remote(dyw.at[xp], dyw.at[xp], y_send.at[2], y_recv.at[2], xdev(RELAY))
+        remote(dyw.at[x], dyw.at[xp], y_send.at[o // 2], y_recv.at[o // 2], xdev(o)).wait_recv()
+
+    def y_relay(o):
+        block = dyw.at[lax.rem(x + o, NX), pl.ds(o // 2 * (BLK // 2), BLK // 2)]
+        return remote(block, block, y_send.at[2 + o // 2], y_recv.at[2 + o // 2], xdev(NX - o))
+
+    def y_relay_wait(o):
+        block = dyw.at[lax.rem(x + 2, NX), pl.ds(o // 2 * (BLK // 2), BLK // 2)]
+        remote(block, block, y_send.at[2 + o // 2], y_recv.at[2 + o // 2], xdev(NX - o)).wait_recv()
 
     mine = pl.ds(pl.multiple_of(FEAT * x, 32), FEAT)
     loads[0].wait()
@@ -183,7 +181,7 @@
     for o in order:
         x_copy(2, o, qsend, qwin, 0).start()
     loads[3].wait()
-    for o in (NX - RELAY, RELAY)[::-1]:
+    for o in (1, 3):
         y_copy(o).start()
     kwin[REACH + x] = ksend[mine, :]
     vwin[REACH + x] = vsend[mine, :]
@@ -239,8 +237,9 @@
             z_down(t, xp + 1, win).wait_recv()
     lax.fori_loop(0, REACH, unpack_kv, 0)
     lax.fori_loop(REACH + NX, SLOTS, unpack_kv, 0)
-    y_wait(NX - RELAY)
-    y_relay().start()
+    for o in (1, 3):
+        y_wait(o)
+        y_relay(o).start()
 
     first = (NX * z - REACH) * BLK
     rows = lax.broadcasted_iota(jnp.int32, (BLK, QG), 0)
@@ -287,25 +286,15 @@
             att[h, :, g * QG : (g + 1) * QG] = mixed.astype(BF16)
         return carry
 
-    lax.fori_loop(0, HPD, forward, 0)
-
-    loads[4].wait()
-    y_wait(RELAY)
-    xp2 = lax.rem(x + 2, NX)
-    remote(dyw.at[xp2], dyw.at[xp2], y_send.at[2], y_recv.at[2], xdev(RELAY)).wait_recv()
-    for b in range(NX):
-        d_blk = dot_nt(wbuf[...], dyw[b])
-        for h in range(HPD):
-            dt[h, :, b * BLK : (b + 1) * BLK] = d_blk[h * HD : (h + 1) * HD].astype(BF16)
-    wp[...] = jnp.zeros_like(wp)
-    dy_all = dyw[...].reshape(OWN, D)
-    for h in range(HPD):
-        wp[h, 0:HD, :] = dot_nn(att[h], dy_all).astype(BF16)
-
     far = pl.ds(pl.multiple_of(CSTEP * (1 - core), BLK), CHUNK)
     near = pl.ds(pl.multiple_of(CSTEP * core, BLK), CHUNK)
     s0_copy = remote(wp.at[:, :, far], r0, s0_send, s0_recv, twin)
-    s0_copy.start()
+
+    def s0_begin():
+        dy_all = dyw[...].reshape(OWN, D)
+        for h in range(HPD):
+            wp[h, 0:HD, :] = dot_nn(att[h], dy_all).astype(BF16)
+        s0_copy.start()
 
     def s1_copy(o):
         return remote(
@@ -339,10 +328,8 @@
             def _():
                 r2[r] = s2[r]
 
-    def s3_copy(t, d):
-        return remote(
-            s3.at[t], r3.at[core, z], s3_send.at[t, d], s3_recv.at[core, z], (jnp.int32(d), owner[t])
-        )
+    def s3_copy(t):
+        return remote(s3.at[t], h5.at[z], s3_send.at[t], s3_recv.at[z], (dp, owner[t]))
 
     def s3_begin():
         @pl.when(reducer)
@@ -361,15 +348,41 @@
             for t in range(2):
                 s3[t] = tot[t * ROWS : t * ROWS + PADR, :].astype(BF16)
             for t in range(2):
-                for d in range(NDP):
-
-                    @pl.when(jnp.logical_not(is_me(t, d)))
-                    def _():
-                        s3_copy(t, d).start()
-
-                    @pl.when(is_me(t, d))
-                    def _():
-                        pltpu.make_async_copy(s3.at[t], r3.at[core, z], o_sem).start()
+
+                @pl.when(owner[t] != seq)
+                def _():
+                    s3_copy(t).start()
+
+                @pl.when(owner[t] == seq)
+                def _():
+                    h5[z] = s3[t]
+
+    def s4_copy(o):
+        return remote(h5, h5, s4_send.at[o], s4_recv.at[NY - o], ydev(o))
+
+    def s4_begin():
+        @pl.when(collector)
+        def _():
+            for r in range(NRED):
+
+                @pl.when(jnp.logical_not(is_source(r)))
+                def _():
+                    remote(s3.at[0], h5.at[r], s3_send.at[0], s3_recv.at[r], (dp, NX * r + src_x)).wait_recv()
+
+            for o in order:
+                s4_copy(o).start()
+
+    s5_copy = remote(h5, r3.at[core], s5_send, s5_recv, twin)
+
+    def s5_begin():
+        for o in order:
+
+            @pl.when(lax.rem(y + o, NY) == src_y)
+            def _():
+                remote(h5, h5, s4_send.at[o], s4_recv.at[o], ydev(o)).wait_recv()
+
+        s5_copy.start()
+        r3[core] = h5[...]
 
     def backward(h, i, pair):
         feats = slice(i * HD, (i + 1) * HD)
@@ -456,28 +469,29 @@
                 stage[p, b] = val.astype(BF16)
                 g_start(1 + t, p, b)
 
+    wp[...] = jnp.zeros_like(wp)
+    lax.fori_loop(0, HPD, forward, 0)
+    for o in (1, 3):
+        y_relay_wait(o)
+    s0_begin()
+    loads[4].wait()
+    for b in range(NX):
+        d_blk = dot_nt(wbuf[...], dyw[b])
+        for h in range(HPD):
+            dt[h, :, b * BLK : (b + 1) * BLK] = d_blk[h * HD : (h + 1) * HD].astype(BF16)
+    s1_begin()
     backward(0, 0, 0)
-    s1_begin()
     backward(1, 1, 0)
     halo_send(0)
     backward(2, 0, 1)
+    s2_begin()
     backward(3, 1, 1)
     halo_send(1)
-    s2_begin()
+    s3_begin()
     halo_add(0)
-    s3_begin()
+    s4_begin()
     halo_add(1)
-
-    for c in range(NCORE):
-        for r in range(NRED):
-
-            @pl.when(is_source(c, r))
-            def _():
-                pltpu.make_async_copy(s3.at[0], r3.at[c, r], o_sem).wait()
-
-            @pl.when(jnp.logical_not(is_source(c, r)))
-            def _():
-                remote(s3.at[0], r3.at[c, r], s3_send.at[0, 0], s3_recv.at[c, r], source(c, r)).wait_recv()
+    s5_begin()
 
     for t in range(3):
         for p in range(PAIRS):
@@ -486,9 +500,9 @@
         x_copy(0, o, ksend, kwin, REACH).wait_send()
         x_copy(1, o, vsend, vwin, REACH).wait_send()
         x_copy(2, o, qsend, qwin, 0).wait_send()
-    y_copy(RELAY).wait_send()
-    y_copy(NX - RELAY).wait_send()
-    y_relay().wait_send()
+    for o in (1, 3):
+        y_copy(o).wait_send()
+        y_relay(o).wait_send()
     for t, win in ((0, kwin), (1, vwin)):
         for xp in range(REACH):
             z_up(t, xp, win).wait_send()
@@ -517,14 +531,17 @@
     @pl.when(reducer)
     def _():
         for t in range(2):
-            for d in range(NDP):
-
-                @pl.when(jnp.logical_not(is_me(t, d)))
-                def _():
-                    s3_copy(t, d).wait_send()
-
-
-RELAY = NX - 1
+
+            @pl.when(owner[t] != seq)
+            def _():
+                s3_copy(t).wait_send()
+
+    @pl.when(collector)
+    def _():
+        for o in order:
+            s4_copy(o).wait_send()
+
+    remote(h5, r3.at[1 - core], s5_send, s5_recv, twin).wait()
 
 
 def main_call(lengths, queries, keys, values, out_grad, out_weight):
@@ -549,45 +566,51 @@
             b16(PAIRS, 2 * REACH, PF, BLK), b16(PAIRS, 2 * REACH, PF, BLK),
             b16(PAIRS, NX, PF, BLK), b16(PAIRS, NX, PF, BLK),
             b16(HPD, PADW, D), b16(HPD, PADW, CHUNK), b16(HPD, PADW, CHUNK), b16(NY, PADW, CHUNK),
-            b16(NRED, PADW, BLK), b16(NZ, PADW, BLK), f32(PADW + 8, BLK), b16(2, PADR, BLK),
-            dma((5,)), dma((3, NX)), dma((3, NX)), dma((NX,)), dma((NX,)), dma((2, 2, NX)), dma((2, 2, NX)),
+            b16(NRED, PADW, BLK), b16(NZ, PADW, BLK), f32(PADW + 8, BLK), b16(2, PADR, BLK), b16(NRED, PADR, BLK),
+            dma((5,)), dma((3, NX)), dma((3, NX)), dma((4,)), dma((4,)), dma((2, 2, NX)), dma((2, 2, NX)),
             dma((2, PAIRS, 2)), dma((2, PAIRS, 2)), dma((3, PAIRS, NX)), dma((3, PAIRS, NX)),
-            dma, dma, dma((NY,)), dma((NY,)), dma((NRED,)), dma((NZ,)), dma((2, NDP)), dma((NCORE, NRED)), dma,
+            dma, dma, dma((NY,)), dma((NY,)), dma((NRED,)), dma((NZ,)), dma((2,)), dma((NRED,)),
+            dma((NY,)), dma((NY,)), dma, dma,
         ],
         compiler_params=pltpu.CompilerParams(
-            collective_id=0, has_side_effects=True, vmem_limit_bytes=52 * 2**20
+            collective_id=0, has_side_effects=True, vmem_limit_bytes=60 * 2**20
         ),
         name="attention_backward",
     )(lengths, queries, keys, values, out_grad, out_weight)
 
 
-PART = 3 * BLK
-
-
-def finish_kernel(rq, rk, rv, rw, gq, gk, gv, gw):
-    for src, dst in ((rq, gq), (rk, gk), (rv, gv)):
-        for i in range(PART // BLK):
-            tile = src[i * BLK : (i + 1) * BLK, :].astype(F32)
-            dst[0, :, i * BLK : (i + 1) * BLK] = tile.T
-
-    @pl.when(pl.program_id(0) == 0)
-    def _():
-        for c in range(NCORE):
-            for r in range(NRED):
-                col = c * CSTEP + r * BLK
-                gw[:, col : col + BLK] = rw[c, r, 0:ROWS, :].astype(F32)
+def finish_kernel(rq, rk, rv, rw, gq, gk, gv, gw, inb, outb, wbuf, i_sem, o_sem):
+    gets = [pltpu.make_async_copy(r, inb.at[t], i_sem.at[t]) for t, r in enumerate((rq, rk, rv))]
+    puts = [pltpu.make_async_copy(outb.at[t], g.at[0], o_sem.at[t]) for t, g in enumerate((gq, gk, gv))]
+    for copy in gets:
+        copy.start()
+    for t in range(3):
+        gets[t].wait()
+        for i in range(D // BLK):
+            outb[t, :, i * BLK : (i + 1) * BLK] = inb[t, i * BLK : (i + 1) * BLK, :].astype(F32).T
+        puts[t].start()
+    for c in range(NCORE):
+        for r in range(NRED):
+            col = c * CSTEP + r * BLK
+            wbuf[:, col : col + BLK] = rw[c, r, 0:ROWS, :].astype(F32)
+    last = pltpu.make_async_copy(wbuf, gw, o_sem.at[3])
+    last.start()
+    for copy in puts:
+        copy.wait()
+    last.wait()
 
 
 def finish(rq, rk, rv, rw):
     grad = jax.ShapeDtypeStruct((1, BLK, D), F32)
-    wide = pl.BlockSpec((PART, BLK), lambda i: (i, 0))
-    tall = pl.BlockSpec((1, BLK, PART), lambda i: (0, 0, i))
     return pl.pallas_call(
         finish_kernel,
-        grid=(D // PART,),
         out_shape=(grad, grad, grad, jax.ShapeDtypeStruct((ROWS, D), F32)),
-        in_specs=[wide] * 3 + [pl.BlockSpec((NCORE, NRED, PADR, BLK), lambda i: (0, 0, 0, 0))],
-        out_specs=(tall, tall, tall, pl.BlockSpec((ROWS, D), lambda i: (0, 0))),
+        in_specs=[HB] * 3 + [VM],
+        out_specs=(HB,) * 4,
+        scratch_shapes=[
+            pltpu.VMEM((3, D, BLK), BF16), pltpu.VMEM((3, BLK, D), F32), pltpu.VMEM((ROWS, D), F32),
+            pltpu.SemaphoreType.DMA((3,)), pltpu.SemaphoreType.DMA((4,)),
+        ],
         name="outputs",
     )(*[r.reshape(D, BLK) for r in (rq, rk, rv)], rw)
 

time: 84.8 us -> 69.7 us (0.82)
  the two profiles are of different devices: /device:TPU:155 before, /device:TPU:8 now
where the time goes in v3:
time: 69.7 us; the launch traced here: 69.4 us
  Pallas kernels  68.7 us (99%)
    pallas_call x1, Pallas kernels, main_call(): pl.pallas_call(main_kernel, out_shape=(back, back, back, jax.ShapeDtypeSt...  65.4 us
    pallas_call x1, Pallas kernels, finish(): pl.pallas_call(finish_kernel, out_shape=(grad, grad, grad, jax.ShapeDtype...  3.35 us

profile of v3, /device:TPU:8, one launch (start us, length us, event | category | flops | bytes accessed | tf_op | source)
XLA Modules:
  0.0 69.4 jit_solution(3631823956066607740)
XLA Ops:
  0.6 65.4 %attention_backward.1 = (bf16[4,288,128]{2,1,0:T(8,128)(2,1)}, bf16[4,288,128]{2,1,0:T(8,128)(2,1)}, bf16[4,288,128]{2,1,0:T(8,128)(2,1)}, bf16[2,5,48,128]{3,2,1,0:T(8,128)(2,1)}) custom-call(s32[1,20]{1,0:T(1,128)} %len_ref.1, bf16[1,128,1152]{2,1,0:T(8,128)(2,1)} %q_hbm.1, bf16[1,128,1152]{2,1,0:T(8,128)(2,1)} %k_hbm.1, bf16[1,128,1152]{2,1,0:T(8,128)(2,1)} %v_hbm.1, ...), custom_call_target="tpu_custom_call" | custom-call | tf_op jit(solution)/shard_map/attention_backward/pallas_call | solution.py:552
  66.0 3.3 %outputs.1 = (f32[1,128,1152]{2,1,0:T(8,128)}, f32[1,128,1152]{2,1,0:T(8,128)}, f32[1,128,1152]{2,1,0:T(8,128)}, f32[36,1152]{1,0:T(8,128)}) custom-call(bf16[1152,128]{1,0:T(8,128)(2,1)} %bitcast.3, bf16[1152,128]{1,0:T(8,128)(2,1)} %bitcast.4, bf16[1152,128]{1,0:T(8,128)(2,1)} %bitcast.5, bf16[2,5,48,128]{3,2,1,0:T(8,128)(2,1)} %get-tuple-element.11.rw), custom_call_target="tpu_custom_call" | custom-call | tf_op jit(solution)/shard_map/outputs/pallas_call | solution.py:605

commit v4 on v3

--- a/solution.py
+++ b/solution.py
@@ -30,6 +30,7 @@
 KG = QG + 2 * REACH * BLK
 NCH = KG // BLK
 PAIRS = HPD // 2
+PART = 3 * BLK
 PF = 2 * HD
 PADW = 80
 CHUNK = 640
@@ -151,20 +152,26 @@
         xp = lax.rem(x + o, NX)
         remote(part(src, xp), win.at[base + xp], x_send.at[t, o], x_recv.at[t, o], xdev(o)).wait_recv()
 
-    def y_copy(o):
-        return remote(dyw.at[x], dyw.at[x], y_send.at[o // 2], y_recv.at[(NX - o) // 2], xdev(o))
-
-    def y_wait(o):
-        xp = lax.rem(x + o, NX)
-        remote(dyw.at[x], dyw.at[xp], y_send.at[o // 2], y_recv.at[o // 2], xdev(o)).wait_recv()
+    def y_rows(o, part):
+        return pl.ds((o // 2 if part == 0 else 1 - o // 2) * (BLK // 2), BLK // 2)
+
+    def y_copy(o, part):
+        block = dyw.at[x, y_rows(NX - o, part)]
+        there = (NX - o) // 2 * 2 + part
+        return remote(block, block, y_send.at[o // 2 * 2 + part], y_recv.at[there], xdev(o))
+
+    def y_wait(o, part):
+        block = dyw.at[lax.rem(x + o, NX), y_rows(o, part)]
+        here = o // 2 * 2 + part
+        remote(block, block, y_send.at[here], y_recv.at[here], xdev(o)).wait_recv()
 
     def y_relay(o):
-        block = dyw.at[lax.rem(x + o, NX), pl.ds(o // 2 * (BLK // 2), BLK // 2)]
-        return remote(block, block, y_send.at[2 + o // 2], y_recv.at[2 + o // 2], xdev(NX - o))
+        block = dyw.at[lax.rem(x + o, NX), y_rows(o, 0)]
+        return remote(block, block, y_send.at[4 + o // 2], y_recv.at[4 + o // 2], xdev(NX - o))
 
     def y_relay_wait(o):
-        block = dyw.at[lax.rem(x + 2, NX), pl.ds(o // 2 * (BLK // 2), BLK // 2)]
-        remote(block, block, y_send.at[2 + o // 2], y_recv.at[2 + o // 2], xdev(NX - o)).wait_recv()
+        block = dyw.at[lax.rem(x + 2, NX), y_rows(o, 0)]
+        remote(block, block, y_send.at[4 + o // 2], y_recv.at[4 + o // 2], xdev(NX - o)).wait_recv()
 
     mine = pl.ds(pl.multiple_of(FEAT * x, 32), FEAT)
     loads[0].wait()
@@ -181,8 +188,9 @@
     for o in order:
         x_copy(2, o, qsend, qwin, 0).start()
     loads[3].wait()
-    for o in (1, 3):
-        y_copy(o).start()
+    for n in range(2):
+        for o in (1, 3):
+            y_copy(o, n).start()
     kwin[REACH + x] = ksend[mine, :]
     vwin[REACH + x] = vsend[mine, :]
     qwin[x] = qsend[mine, :]
@@ -238,7 +246,7 @@
     lax.fori_loop(0, REACH, unpack_kv, 0)
     lax.fori_loop(REACH + NX, SLOTS, unpack_kv, 0)
     for o in (1, 3):
-        y_wait(o)
+        y_wait(o, 0)
         y_relay(o).start()
 
     first = (NX * z - REACH) * BLK
@@ -283,7 +291,7 @@
                     s_scr[g, c * BLK : (c + 1) * BLK, :] * inv
                 ).astype(BF16)
             mixed = dot_nn(vt[h, :, g * QG : g * QG + KG], p_scr[g, h])
-            att[h, :, g * QG : (g + 1) * QG] = mixed.astype(BF16)
+            att[pl.ds(pl.multiple_of(h * HD, 8), HD), g * QG : (g + 1) * QG] = mixed
         return carry
 
     far = pl.ds(pl.multiple_of(CSTEP * (1 - core), BLK), CHUNK)
@@ -291,9 +299,12 @@
     s0_copy = remote(wp.at[:, :, far], r0, s0_send, s0_recv, twin)
 
     def s0_begin():
-        dy_all = dyw[...].reshape(OWN, D)
-        for h in range(HPD):
-            wp[h, 0:HD, :] = dot_nn(att[h], dy_all).astype(BF16)
+        attended = att[...].astype(BF16)
+        for i in range(D // PART):
+            cols = slice(i * PART, (i + 1) * PART)
+            share = dot_nn(attended, dyw[:, :, cols].reshape(OWN, PART))
+            for h in range(HPD):
+                wp[h, 0:HD, cols] = share[h * HD : (h + 1) * HD].astype(BF16)
         s0_copy.start()
 
     def s1_copy(o):
@@ -389,7 +400,8 @@
         for g in range(NG):
             cols = slice(g * QG, (g + 1) * QG)
             q_blk, d_blk, p_all = qt[h, :, cols], dt[h, :, cols], p_scr[g, h]
-            delta = jnp.sum(d_blk.astype(F32) * att[h, :, cols].astype(F32), axis=0, keepdims=True)
+            mixed = att[h * HD : (h + 1) * HD, cols].astype(BF16).astype(F32)
+            delta = jnp.sum(d_blk.astype(F32) * mixed, axis=0, keepdims=True)
             for c in range(NCH):
                 keys = slice(g * QG + c * BLK, g * QG + (c + 1) * BLK)
                 dp_c = dot_nn(vr[h, keys, :], d_blk)
@@ -472,23 +484,25 @@
     wp[...] = jnp.zeros_like(wp)
     lax.fori_loop(0, HPD, forward, 0)
     for o in (1, 3):
+        y_wait(o, 1)
+    for o in (1, 3):
         y_relay_wait(o)
     s0_begin()
     loads[4].wait()
-    for b in range(NX):
-        d_blk = dot_nt(wbuf[...], dyw[b])
+    for g in range(NG):
+        d_blk = dot_nt(wbuf[...], dyw[g * 2 : g * 2 + 2].reshape(QG, D))
         for h in range(HPD):
-            dt[h, :, b * BLK : (b + 1) * BLK] = d_blk[h * HD : (h + 1) * HD].astype(BF16)
+            dt[h, :, g * QG : (g + 1) * QG] = d_blk[h * HD : (h + 1) * HD].astype(BF16)
     s1_begin()
     backward(0, 0, 0)
     backward(1, 1, 0)
     halo_send(0)
     backward(2, 0, 1)
+    backward(3, 1, 1)
     s2_begin()
-    backward(3, 1, 1)
     halo_send(1)
+    halo_add(0)
     s3_begin()
-    halo_add(0)
     s4_begin()
     halo_add(1)
     s5_begin()
@@ -501,7 +515,8 @@
         x_copy(1, o, vsend, vwin, REACH).wait_send()
         x_copy(2, o, qsend, qwin, 0).wait_send()
     for o in (1, 3):
-        y_copy(o).wait_send()
+        y_copy(o, 0).wait_send()
+        y_copy(o, 1).wait_send()
         y_relay(o).wait_send()
     for t, win in ((0, kwin), (1, vwin)):
         for xp in range(REACH):
@@ -560,14 +575,14 @@
             b16(SLOTS, FEAT, BLK), b16(SLOTS, FEAT, BLK), b16(NX, FEAT, BLK),
             b16(HPD, HD, OWN), b16(HPD, HD, WIDE), b16(HPD, HD, WIDE), b16(HPD, WIDE, HD), b16(HPD, WIDE, HD),
             b16(HPD, HD, OWN),
-            f32(NG, KG, QG), b16(NG, HPD, KG, QG), b16(NG, KG, QG), b16(HPD, HD, OWN),
+            f32(NG, KG, QG), b16(NG, HPD, KG, QG), b16(NG, KG, QG), f32(FEAT, OWN),
             f32(PAIRS, PF, OWN), f32(PAIRS, PF, WIDE), f32(PAIRS, PF, WIDE),
             b16(PAIRS, NX, PF, BLK), b16(PAIRS, 2 * REACH, PF, BLK), b16(PAIRS, 2 * REACH, PF, BLK),
             b16(PAIRS, 2 * REACH, PF, BLK), b16(PAIRS, 2 * REACH, PF, BLK),
             b16(PAIRS, NX, PF, BLK), b16(PAIRS, NX, PF, BLK),
             b16(HPD, PADW, D), b16(HPD, PADW, CHUNK), b16(HPD, PADW, CHUNK), b16(NY, PADW, CHUNK),
             b16(NRED, PADW, BLK), b16(NZ, PADW, BLK), f32(PADW + 8, BLK), b16(2, PADR, BLK), b16(NRED, PADR, BLK),
-            dma((5,)), dma((3, NX)), dma((3, NX)), dma((4,)), dma((4,)), dma((2, 2, NX)), dma((2, 2, NX)),
+            dma((5,)), dma((3, NX)), dma((3, NX)), dma((6,)), dma((6,)), dma((2, 2, NX)), dma((2, 2, NX)),
             dma((2, PAIRS, 2)), dma((2, PAIRS, 2)), dma((3, PAIRS, NX)), dma((3, PAIRS, NX)),
             dma, dma, dma((NY,)), dma((NY,)), dma((NRED,)), dma((NZ,)), dma((2,)), dma((NRED,)),
             dma((NY,)), dma((NY,)), dma, dma,

time: 69.7 us -> 67.1 us (0.963)
  Pallas kernels: 68.7 us -> 66 us
    pallas_call x1, Pallas kernels: 65.4 us -> 62.7 us  [main_call(): pl.pallas_call(main_kernel, out_shape=(back, back, back, jax.ShapeDtypeSt...]
where the time goes in v4:
time: 67.1 us; the launch traced here: 66.7 us
  Pallas kernels  66 us (98%)
    pallas_call x1, Pallas kernels, main_call(): pl.pallas_call(main_kernel, out_shape=(back, back, back, jax.ShapeDtypeSt...  62.7 us
    pallas_call x1, Pallas kernels, finish(): pl.pallas_call(finish_kernel, out_shape=(grad, grad, grad, jax.ShapeDtype...  3.35 us

profile of v4, /device:TPU:8, one launch (start us, length us, event | category | flops | bytes accessed | tf_op | source)
XLA Modules:
  0.0 66.7 jit_solution(17410239174378447760)
XLA Ops:
  0.6 62.7 %attention_backward.1 = (bf16[4,288,128]{2,1,0:T(8,128)(2,1)}, bf16[4,288,128]{2,1,0:T(8,128)(2,1)}, bf16[4,288,128]{2,1,0:T(8,128)(2,1)}, bf16[2,5,48,128]{3,2,1,0:T(8,128)(2,1)}) custom-call(s32[1,20]{1,0:T(1,128)} %len_ref.1, bf16[1,128,1152]{2,1,0:T(8,128)(2,1)} %q_hbm.1, bf16[1,128,1152]{2,1,0:T(8,128)(2,1)} %k_hbm.1, bf16[1,128,1152]{2,1,0:T(8,128)(2,1)} %v_hbm.1, ...), custom_call_target="tpu_custom_call" | custom-call | tf_op jit(solution)/shard_map/attention_backward/pallas_call | solution.py:567
  63.3 3.3 %outputs.1 = (f32[1,128,1152]{2,1,0:T(8,128)}, f32[1,128,1152]{2,1,0:T(8,128)}, f32[1,128,1152]{2,1,0:T(8,128)}, f32[36,1152]{1,0:T(8,128)}) custom-call(bf16[1152,128]{1,0:T(8,128)(2,1)} %bitcast.3, bf16[1152,128]{1,0:T(8,128)(2,1)} %bitcast.4, bf16[1152,128]{1,0:T(8,128)(2,1)} %bitcast.5, bf16[2,5,48,128]{3,2,1,0:T(8,128)(2,1)} %get-tuple-element.11.rw), custom_call_target="tpu_custom_call" | custom-call | tf_op jit(solution)/shard_map/outputs/pallas_call | solution.py:620

commit v5 on v4

--- a/solution.py
+++ b/solution.py
@@ -226,8 +226,11 @@
             if r_out is not None:
                 r_out[h, cols, :] = piece.T.astype(BF16)
 
-    def unpack_kv(slot, carry):
+    def unpack_k(slot, carry):
         unpack(kwin, slot, kt, kr)
+        return carry
+
+    def unpack_v(slot, carry):
         unpack(vwin, slot, vt, vr)
         return carry
 
@@ -235,19 +238,18 @@
         unpack(qwin, slot, qt, None)
         return carry
 
-    lax.fori_loop(REACH, REACH + NX, unpack_kv, 0)
-    for o in order:
-        x_wait(2, o, qsend, qwin, 0)
-    lax.fori_loop(0, NX, unpack_q, 0)
-    for t, win in ((0, kwin), (1, vwin)):
+    def halo_wait(t, win):
         for xp in range(REACH):
             z_up(t, xp, win).wait_recv()
             z_down(t, xp + 1, win).wait_recv()
-    lax.fori_loop(0, REACH, unpack_kv, 0)
-    lax.fori_loop(REACH + NX, SLOTS, unpack_kv, 0)
-    for o in (1, 3):
-        y_wait(o, 0)
-        y_relay(o).start()
+
+    lax.fori_loop(REACH, REACH + NX, unpack_k, 0)
+    halo_wait(0, kwin)
+    lax.fori_loop(0, REACH, unpack_k, 0)
+    lax.fori_loop(REACH + NX, SLOTS, unpack_k, 0)
+    for o in order:
+        x_wait(2, o, qsend, qwin, 0)
+    lax.fori_loop(0, NX, unpack_q, 0)
 
     first = (NX * z - REACH) * BLK
     rows = lax.broadcasted_iota(jnp.int32, (BLK, QG), 0)
@@ -290,6 +292,10 @@
                 p_scr[g, h, c * BLK : (c + 1) * BLK, :] = (
                     s_scr[g, c * BLK : (c + 1) * BLK, :] * inv
                 ).astype(BF16)
+        return carry
+
+    def mix(h, carry):
+        for g in range(NG):
             mixed = dot_nn(vt[h, :, g * QG : g * QG + KG], p_scr[g, h])
             att[pl.ds(pl.multiple_of(h * HD, 8), HD), g * QG : (g + 1) * QG] = mixed
         return carry
@@ -482,7 +488,16 @@
                 g_start(1 + t, p, b)
 
     wp[...] = jnp.zeros_like(wp)
-    lax.fori_loop(0, HPD, forward, 0)
+    lax.fori_loop(0, PAIRS, forward, 0)
+    for o in (1, 3):
+        y_wait(o, 0)
+        y_relay(o).start()
+    lax.fori_loop(PAIRS, HPD, forward, 0)
+    lax.fori_loop(REACH, REACH + NX, unpack_v, 0)
+    halo_wait(1, vwin)
+    lax.fori_loop(0, REACH, unpack_v, 0)
+    lax.fori_loop(REACH + NX, SLOTS, unpack_v, 0)
+    lax.fori_loop(0, HPD, mix, 0)
     for o in (1, 3):
         y_wait(o, 1)
     for o in (1, 3):
@@ -500,9 +515,9 @@
     backward(2, 0, 1)
     backward(3, 1, 1)
     s2_begin()
+    s3_begin()
     halo_send(1)
     halo_add(0)
-    s3_begin()
     s4_begin()
     halo_add(1)
     s5_begin()

time: 67.1 us -> 64.6 us (0.963)
  Pallas kernels: 66 us -> 63.7 us
    pallas_call x1, Pallas kernels: 62.7 us -> 60.4 us  [main_call(): pl.pallas_call(main_kernel, out_shape=(back, back, back, jax.ShapeDtypeSt...]
where the time goes in v5:
time: 64.6 us; the launch traced here: 64.4 us
  Pallas kernels  63.7 us (99%)
    pallas_call x1, Pallas kernels, main_call(): pl.pallas_call(main_kernel, out_shape=(back, back, back, jax.ShapeDtypeSt...  60.4 us
    pallas_call x1, Pallas kernels, finish(): pl.pallas_call(finish_kernel, out_shape=(grad, grad, grad, jax.ShapeDtype...  3.35 us

profile of v5, /device:TPU:8, one launch (start us, length us, event | category | flops | bytes accessed | tf_op | source)
XLA Modules:
  0.0 64.4 jit_solution(4139534616476804102)
XLA Ops:
  0.6 60.4 %attention_backward.1 = (bf16[4,288,128]{2,1,0:T(8,128)(2,1)}, bf16[4,288,128]{2,1,0:T(8,128)(2,1)}, bf16[4,288,128]{2,1,0:T(8,128)(2,1)}, bf16[2,5,48,128]{3,2,1,0:T(8,128)(2,1)}) custom-call(s32[1,20]{1,0:T(1,128)} %len_ref.1, bf16[1,128,1152]{2,1,0:T(8,128)(2,1)} %q_hbm.1, bf16[1,128,1152]{2,1,0:T(8,128)(2,1)} %k_hbm.1, bf16[1,128,1152]{2,1,0:T(8,128)(2,1)} %v_hbm.1, ...), custom_call_target="tpu_custom_call" | custom-call | tf_op jit(solution)/shard_map/attention_backward/pallas_call | solution.py:582
  61.0 3.3 %outputs.1 = (f32[1,128,1152]{2,1,0:T(8,128)}, f32[1,128,1152]{2,1,0:T(8,128)}, f32[1,128,1152]{2,1,0:T(8,128)}, f32[36,1152]{1,0:T(8,128)}) custom-call(bf16[1152,128]{1,0:T(8,128)(2,1)} %bitcast.3, bf16[1152,128]{1,0:T(8,128)(2,1)} %bitcast.4, bf16[1152,128]{1,0:T(8,128)(2,1)} %bitcast.5, bf16[2,5,48,128]{3,2,1,0:T(8,128)(2,1)} %get-tuple-element.11.rw), custom_call_target="tpu_custom_call" | custom-call | tf_op jit(solution)/shard_map/outputs/pallas_call | solution.py:635

commit v6 on v5

--- a/solution.py
+++ b/solution.py
@@ -517,8 +517,8 @@
     s2_begin()
     s3_begin()
     halo_send(1)
+    s4_begin()
     halo_add(0)
-    s4_begin()
     halo_add(1)
     s5_begin()
 

time: 64.6 us -> 67.5 us (1.045)
  Pallas kernels: 63.7 us -> 66.7 us
    pallas_call x1, Pallas kernels: 60.4 us -> 63.4 us  [main_call(): pl.pallas_call(main_kernel, out_shape=(back, back, back, jax.ShapeDtypeSt...]
where the time goes in v6:
time: 67.5 us; the launch traced here: 67.3 us
  Pallas kernels  66.7 us (99%)
    pallas_call x1, Pallas kernels, main_call(): pl.pallas_call(main_kernel, out_shape=(back, back, back, jax.ShapeDtypeSt...  63.4 us
    pallas_call x1, Pallas kernels, finish(): pl.pallas_call(finish_kernel, out_shape=(grad, grad, grad, jax.ShapeDtype...  3.35 us

profile of v6, /device:TPU:8, one launch (start us, length us, event | category | flops | bytes accessed | tf_op | source)
XLA Modules:
  0.0 67.3 jit_solution(13406893414603739109)
XLA Ops:
  0.6 63.4 %attention_backward.1 = (bf16[4,288,128]{2,1,0:T(8,128)(2,1)}, bf16[4,288,128]{2,1,0:T(8,128)(2,1)}, bf16[4,288,128]{2,1,0:T(8,128)(2,1)}, bf16[2,5,48,128]{3,2,1,0:T(8,128)(2,1)}) custom-call(s32[1,20]{1,0:T(1,128)} %len_ref.1, bf16[1,128,1152]{2,1,0:T(8,128)(2,1)} %q_hbm.1, bf16[1,128,1152]{2,1,0:T(8,128)(2,1)} %k_hbm.1, bf16[1,128,1152]{2,1,0:T(8,128)(2,1)} %v_hbm.1, ...), custom_call_target="tpu_custom_call" | custom-call | tf_op jit(solution)/shard_map/attention_backward/pallas_call | solution.py:582
  64.0 3.3 %outputs.1 = (f32[1,128,1152]{2,1,0:T(8,128)}, f32[1,128,1152]{2,1,0:T(8,128)}, f32[1,128,1152]{2,1,0:T(8,128)}, f32[36,1152]{1,0:T(8,128)}) custom-call(bf16[1152,128]{1,0:T(8,128)(2,1)} %bitcast.3, bf16[1152,128]{1,0:T(8,128)(2,1)} %bitcast.4, bf16[1152,128]{1,0:T(8,128)(2,1)} %bitcast.5, bf16[2,5,48,128]{3,2,1,0:T(8,128)(2,1)} %get-tuple-element.11.rw), custom_call_target="tpu_custom_call" | custom-call | tf_op jit(solution)/shard_map/outputs/pallas_call | solution.py:635
